TPU v7x, 32 devices: a whole 2x2x4 slice. The times are simulated.
32 devices in a mesh: rep: 4 (over y, x), fsdp: 4 (over z), seq: 2 (over core).
Axes of the slice: x: 2, y: 2, z: 4, core: 2. Of those that a mesh axis runs over, the one named last changes fastest.
Arguments:
- hidden_in: bfloat16 [16384, 1024], P(('rep', 'fsdp', 'seq')), may hold values from -6 to 6
- norm1_gain: float32 [1024], replicated, may hold values from 0.5 to 1.5
- w_z: bfloat16 [1024, 1536], P(('fsdp', 'seq')), may hold values from -0.1875 to 0.1875
- w_xbc: bfloat16 [1024, 1792], P(('fsdp', 'seq')), may hold values from -0.1875 to 0.1875
- w_dt: bfloat16 [1024, 24], P(('fsdp', 'seq')), may hold values from -0.1875 to 0.1875
- conv_w: float32 [4, 1792], replicated, may hold values from -0.6 to 0.6
- conv_b: float32 [1792], replicated, may hold values from -0.5 to 0.5
- dt_bias: float32 [24], replicated, may hold values from -1 to 0.5
- a_log: float32 [24], replicated, may hold values from -6.9 to -3
- d_skip: float32 [24], replicated, may hold values from 0.5 to 1.5
- ssm_gain: float32 [1536], replicated, may hold values from 0.5 to 1.5
- w_ssm_out: bfloat16 [1536, 1024], P(None, ('fsdp', 'seq')), may hold values from -0.15625 to 0.15625
- w_q: bfloat16 [1024, 512], P(('fsdp', 'seq')), may hold values from -0.1875 to 0.1875
- key_weight: bfloat16 [1024, 128], P(('fsdp', 'seq')), may hold values from -0.1875 to 0.1875
- value_weight: bfloat16 [1024, 128], P(('fsdp', 'seq')), may hold values from -0.1875 to 0.1875
- w_o: bfloat16 [512, 1024], P(None, ('fsdp', 'seq')), may hold values from -0.75 to 0.75
- norm2_gain: float32 [1024], replicated, may hold values from 0.5 to 1.5
- w_gate: bfloat16 [1024, 2048], P(('fsdp', 'seq')), may hold values from -0.1875 to 0.1875
- w_up: bfloat16 [1024, 2048], P(('fsdp', 'seq')), may hold values from -0.1875 to 0.1875
- w_down: bfloat16 [2048, 1024], P(None, ('fsdp', 'seq')), may hold values from -0.125 to 0.125
- grad_out: bfloat16 [16384, 1024], P(('rep', 'fsdp', 'seq')), may hold values from -6 to 6
Outputs:
- out_hidden: bfloat16 [16384, 1024], P(('rep', 'fsdp', 'seq'))
- grad_hidden: float32 [16384, 1024], P(('rep', 'fsdp', 'seq'))
- grad_norm1_gain: float32 [1024], replicated
- grad_w_z: float32 [1024, 1536], P(('fsdp', 'seq'))
- grad_w_xbc: float32 [1024, 1792], P(('fsdp', 'seq'))
- grad_w_dt: float32 [1024, 24], P(('fsdp', 'seq'))
- grad_conv_w: float32 [4, 1792], replicated
- grad_conv_b: float32 [1792], replicated
- grad_dt_bias: float32 [24], replicated
- grad_a_log: float32 [24], replicated
- grad_d_skip: float32 [24], replicated
- grad_ssm_gain: float32 [1536], replicated
- grad_w_ssm_out: float32 [1536, 1024], P(None, ('fsdp', 'seq'))
- grad_w_q: float32 [1024, 512], P(('fsdp', 'seq'))
- grad_w_k: float32 [1024, 128], P(('fsdp', 'seq'))
- grad_w_v: float32 [1024, 128], P(('fsdp', 'seq'))
- grad_w_o: float32 [512, 1024], P(None, ('fsdp', 'seq'))
- grad_norm2_gain: float32 [1024], replicated
- grad_w_gate: float32 [1024, 2048], P(('fsdp', 'seq'))
- grad_w_up: float32 [1024, 2048], P(('fsdp', 'seq'))
- grad_w_down: float32 [2048, 1024], P(None, ('fsdp', 'seq'))
All inputs are finite; a program needn't handle non-finite values.
Results may differ from a plain program's by a relative error of at most 0.018.
Values may be sent and summed in bfloat16 or wider, within the bound.
No kernel may reach another device: no remote copies, remote signals or barrier semaphores. Data moves between devices by JAX's collectives and lax.ppermute only.
A program may use at most 320 MiB of HBM per device.

v0:
```python
import jax
import jax.numpy as jnp
from jax import lax
from jax.sharding import PartitionSpec as P

NH_SSM = 24
HP = 64
NS = 128
KCONV = 4
QUERY_HEADS = 8
KEY_VALUE_HEADS = 2
HEAD_SIZE = 64
BLOCK = 128


HIGH = lax.Precision.HIGHEST
EPS = 1e-06
ROPE_BASE = 10000.0


def from_behind(value, axis, by):
    count = lax.axis_size(axis)
    pairs = [(i, i + by) for i in range(count) if 0 <= i + by < count]
    return lax.ppermute(value, axis, pairs)


def prefix(value, axis, combine, identity):
    count, index = (lax.axis_size(axis), lax.axis_index(axis))
    everything = jax.tree.map(
        lambda part, kind: lax.all_gather(part.astype(kind), axis),
        value,
        (jnp.bfloat16, jnp.bfloat16),
    )
    start = jax.tree.map(
        lambda part, zero: jnp.broadcast_to(jnp.asarray(zero, part.dtype), part.shape),
        value,
        identity,
    )

    def hop(k, before):
        reached = k < index
        new = combine(
            before, jax.tree.map(lambda part, own: part[k].astype(own.dtype), everything, value)
        )
        return jax.tree.map(lambda a, b: jnp.where(reached, a, b), new, before)

    return lax.fori_loop(0, count, hop, start)


def entering(value, axis, join, neutral):
    count = lax.axis_size(axis)
    place = lax.axis_index(axis)
    ahead = count - 1 - place
    gathered = jax.tree.map(
        lambda a, kind: lax.all_gather(a.astype(kind), axis),
        value,
        jax.tree.map(lambda a: jnp.bfloat16 if a.dtype == jnp.float32 else a.dtype, value),
    )
    state = jax.tree.map(lambda a, e: jnp.zeros_like(a) + jnp.asarray(e, a.dtype), value, neutral)

    def one(hop, state):
        source = count - 1 - hop
        return join(
            state,
            jax.tree.map(
                lambda a, own: lax.dynamic_index_in_dim(a, source, 0, False).astype(own.dtype),
                gathered,
                value,
            ),
        )

    return lax.fori_loop(0, ahead, one, state)


def cast_reduced(values):
    return values.astype(jnp.bfloat16)


def apply_projection(left_low, weight):
    return jnp.dot(left_low, weight, preferred_element_type=jnp.float32)


def project_back(grad_low, weight):
    return jnp.einsum("tf,df->td", grad_low, weight, preferred_element_type=jnp.float32)


def weight_term(left_low, grad_low):
    return jnp.einsum("td,tf->df", left_low, grad_low, preferred_element_type=jnp.float32)


def rms_gain(values, gain):
    return values * lax.rsqrt(jnp.mean(values * values, axis=-1, keepdims=True) + EPS) * gain


def rotate(values, positions):
    half_dim = values.shape[-1] // 2
    frequency = ROPE_BASE ** (-jnp.arange(half_dim, dtype=jnp.float32) / half_dim)
    angles = positions.astype(jnp.float32)[:, None] * frequency[None, :]
    cosine = jnp.cos(angles)[:, None, :]
    sine_part = jnp.sin(angles)[:, None, :]
    first_half = values[..., :half_dim]
    second_half = values[..., half_dim:]
    return jnp.concatenate(
        [
            first_half * cosine - second_half * sine_part,
            second_half * cosine + first_half * sine_part,
        ],
        axis=-1,
    )


def conv_piece(extended, conv_w, conv_b, dt_raw, dt_bias, a_log):
    number_of_rows = dt_raw.shape[0]
    total = conv_b[None, :]
    for offset in range(KCONV):
        total = total + conv_w[offset][None, :] * extended[offset : offset + number_of_rows]
    active = jax.nn.silu(total)
    inner = NH_SSM * HP
    values = active[:, :inner].reshape(number_of_rows, NH_SSM, HP)
    b_matrix = active[:, inner : inner + NS]
    c_matrix = active[:, inner + NS :]
    step_size = jax.nn.softplus(dt_raw + dt_bias[None, :])
    log_decay = -step_size * jnp.exp(a_log)[None, :]
    return (values, b_matrix, c_matrix, step_size, log_decay)


def ssd_block(carried, inputs_block):
    values, b_matrix, c_matrix, step_size, log_decay = inputs_block
    number_of_rows = values.shape[0]
    running = jnp.cumsum(log_decay, axis=0)
    causal = (jnp.arange(number_of_rows)[:, None] >= jnp.arange(number_of_rows)[None, :])[
        :, :, None
    ]
    spread = jnp.where(causal, running[:, None, :] - running[None, :, :], 0.0)
    decay = jnp.where(causal, jnp.exp(spread), 0.0)
    inner_cb = jnp.dot(c_matrix, b_matrix.T, precision=HIGH, preferred_element_type=jnp.float32)
    mixing = decay * inner_cb[:, :, None] * step_size[None, :, :]
    within = jnp.einsum("tsh,shp->thp", mixing, values, precision=HIGH)
    from_state = (
        jnp.einsum("tn,hpn->thp", c_matrix, carried, precision=HIGH) * jnp.exp(running)[:, :, None]
    )
    last_row = running[-1]
    weights_tail = jnp.exp(last_row[None, :] - running) * step_size
    new_state = carried * jnp.exp(last_row)[:, None, None] + jnp.einsum(
        "sh,shp,sn->hpn", weights_tail, values, b_matrix, precision=HIGH
    )
    return (new_state, within + from_state)


def ssd_local(values, b_matrix, c_matrix, step_size, log_decay):
    number_of_rows = values.shape[0]
    block_count = number_of_rows // BLOCK
    blocks = (
        values.reshape(block_count, BLOCK, NH_SSM, HP),
        b_matrix.reshape(block_count, BLOCK, NS),
        c_matrix.reshape(block_count, BLOCK, NS),
        step_size.reshape(block_count, BLOCK, NH_SSM),
        log_decay.reshape(block_count, BLOCK, NH_SSM),
    )
    initial = jnp.zeros((NH_SSM, HP, NS), jnp.float32)
    final_state, outputs = lax.scan(jax.checkpoint(ssd_block), initial, blocks)
    return (outputs.reshape(number_of_rows, NH_SSM, HP), final_state, jnp.sum(log_decay, axis=0))


def correction(c_matrix, log_decay, incoming):
    running = jnp.cumsum(log_decay, axis=0)
    return (
        jnp.einsum("tn,hpn->thp", c_matrix, incoming, precision=HIGH) * jnp.exp(running)[:, :, None]
    )


def mamba_tail(y_local, y_extra, values, gate_z, d_skip, ssm_gain):
    number_of_rows = values.shape[0]
    y_all = (y_local + y_extra + d_skip[None, :, None] * values).reshape(
        number_of_rows, NH_SSM * HP
    )
    return rms_gain(y_all * jax.nn.silu(gate_z), ssm_gain)


def swish_product(gate_pre, up_pre):
    return jax.nn.silu(gate_pre) * up_pre


def attention_forward(query_low, keys_low, values_low, query_pos, key_pos):
    number_of_rows = query_low.shape[0]
    grouped_heads = query_low.reshape(
        number_of_rows, KEY_VALUE_HEADS, QUERY_HEADS // KEY_VALUE_HEADS, HEAD_SIZE
    )
    scores = jnp.einsum(
        "tgjd,sgd->gjts", grouped_heads, keys_low, preferred_element_type=jnp.float32
    ) * HEAD_SIZE ** (-0.5)
    allowed = key_pos[None, :] <= query_pos[:, None]
    scores = jnp.where(allowed[None, None], scores, -1e30)
    peak = jnp.max(scores, axis=-1, keepdims=True)
    raised = jnp.exp(scores - peak)
    softened = raised / jnp.sum(raised, axis=-1, keepdims=True)
    probs_low = cast_reduced(softened)
    mixed = jnp.einsum("gjts,sgd->tgjd", probs_low, values_low, preferred_element_type=jnp.float32)
    return (mixed.reshape(number_of_rows, QUERY_HEADS * HEAD_SIZE), softened, probs_low)


def attention_backward(grad_low, query_low, keys_low, values_low, softened, probs_low):
    number_of_rows = query_low.shape[0]
    grouped_heads = query_low.reshape(
        number_of_rows, KEY_VALUE_HEADS, QUERY_HEADS // KEY_VALUE_HEADS, HEAD_SIZE
    )
    grad_grouped = grad_low.reshape(
        number_of_rows, KEY_VALUE_HEADS, QUERY_HEADS // KEY_VALUE_HEADS, HEAD_SIZE
    )
    grad_probs = jnp.einsum(
        "tgjd,sgd->gjts", grad_grouped, values_low, preferred_element_type=jnp.float32
    )
    grad_scores = softened * (grad_probs - jnp.sum(softened * grad_probs, axis=-1, keepdims=True))
    scores_low = cast_reduced(grad_scores)
    scale = HEAD_SIZE ** (-0.5)
    grad_query = (
        jnp.einsum("gjts,sgd->tgjd", scores_low, keys_low, preferred_element_type=jnp.float32)
        * scale
    )
    grad_key = (
        jnp.einsum("gjts,tgjd->sgd", scores_low, grouped_heads, preferred_element_type=jnp.float32)
        * scale
    )
    grad_value = jnp.einsum(
        "gjts,tgjd->sgd", probs_low, grad_grouped, preferred_element_type=jnp.float32
    )
    return (grad_query.reshape(number_of_rows, QUERY_HEADS, HEAD_SIZE), grad_key, grad_value)


def link_states(earlier, later):
    return (earlier[0] * later[0], later[0][:, None, None] * earlier[1] + later[1])


def body(
    hidden_in,
    norm1_gain,
    w_z,
    w_xbc,
    w_dt,
    conv_w,
    conv_b,
    dt_bias,
    a_log,
    d_skip,
    ssm_gain,
    w_ssm_out,
    w_q,
    key_weight,
    value_weight,
    w_o,
    norm2_gain,
    w_gate,
    w_up,
    w_down,
    grad_out,
):
    number_of_rows = hidden_in.shape[0]
    seq_index = lax.axis_index("seq")
    positions = seq_index * number_of_rows + jnp.arange(number_of_rows, dtype=jnp.int32)
    (
        full_z,
        full_xbc,
        full_dt,
        full_out,
        full_q,
        complete_keys,
        full_v,
        full_o,
        full_gate,
        full_up,
        full_down,
    ) = (
        lax.all_gather(w_z, ("fsdp", "seq"), axis=0, tiled=True),
        lax.all_gather(w_xbc, ("fsdp", "seq"), axis=0, tiled=True),
        lax.all_gather(w_dt, ("fsdp", "seq"), axis=0, tiled=True),
        lax.all_gather(w_ssm_out, ("fsdp", "seq"), axis=1, tiled=True),
        lax.all_gather(w_q, ("fsdp", "seq"), axis=0, tiled=True),
        lax.all_gather(key_weight, ("fsdp", "seq"), axis=0, tiled=True),
        lax.all_gather(value_weight, ("fsdp", "seq"), axis=0, tiled=True),
        lax.all_gather(w_o, ("fsdp", "seq"), axis=1, tiled=True),
        lax.all_gather(w_gate, ("fsdp", "seq"), axis=0, tiled=True),
        lax.all_gather(w_up, ("fsdp", "seq"), axis=0, tiled=True),
        lax.all_gather(w_down, ("fsdp", "seq"), axis=1, tiled=True),
    )
    inputs = hidden_in.astype(jnp.float32)
    first_normed, norm1_back = jax.vjp(rms_gain, inputs, norm1_gain)
    first_normed_reduced = cast_reduced(first_normed)
    gate_z = apply_projection(first_normed_reduced, full_z)
    conv_low = cast_reduced(apply_projection(first_normed_reduced, full_xbc))
    dt_raw = apply_projection(first_normed_reduced, full_dt)
    query_raw = apply_projection(first_normed_reduced, full_q).reshape(
        number_of_rows, QUERY_HEADS, HEAD_SIZE
    )
    key_unrotated = apply_projection(first_normed_reduced, complete_keys).reshape(
        number_of_rows, KEY_VALUE_HEADS, HEAD_SIZE
    )
    value_low = cast_reduced(apply_projection(first_normed_reduced, full_v))
    query_rot, query_back = jax.vjp(lambda tensor_in: rotate(tensor_in, positions), query_raw)
    key_rotated, key_pullback_fn = jax.vjp(
        lambda tensor_in: rotate(tensor_in, positions), key_unrotated
    )
    query_low = cast_reduced(query_rot)
    key_reduced = cast_reduced(key_rotated).reshape(number_of_rows, KEY_VALUE_HEADS * HEAD_SIZE)
    keys_gathered, values_gathered = (
        lax.all_gather(key_reduced, "seq", axis=0, tiled=True),
        lax.all_gather(value_low, "seq", axis=0, tiled=True),
    )
    rim_rows = from_behind(conv_low[number_of_rows - (KCONV - 1) :], "seq", 1)
    extended = jnp.concatenate([rim_rows, conv_low], axis=0).astype(jnp.float32)
    (values, b_matrix, c_matrix, step_size, log_decay), conv_back = jax.vjp(
        conv_piece, extended, conv_w, conv_b, dt_raw, dt_bias, a_log
    )
    (y_local, end_state, total_log), ssd_back = jax.vjp(
        ssd_local, values, b_matrix, c_matrix, step_size, log_decay
    )
    decay_total = jnp.exp(total_log)
    prefix_decay, incoming = prefix(
        (decay_total, end_state),
        "seq",
        link_states,
        (jnp.ones_like(decay_total), jnp.zeros_like(end_state)),
    )
    y_extra, corr_back = jax.vjp(correction, c_matrix, log_decay, incoming)
    ssm_normed, tail_back = jax.vjp(mamba_tail, y_local, y_extra, values, gate_z, d_skip, ssm_gain)
    ssm_low = cast_reduced(ssm_normed)
    mamba_out = apply_projection(ssm_low, full_out)
    number_of_keys = keys_gathered.shape[0]
    key_pos = jnp.arange(number_of_keys, dtype=jnp.int32)
    keys_heads = keys_gathered.reshape(number_of_keys, KEY_VALUE_HEADS, HEAD_SIZE)
    values_heads = values_gathered.reshape(number_of_keys, KEY_VALUE_HEADS, HEAD_SIZE)
    attended, softened, probs_low = attention_forward(
        query_low, keys_heads, values_heads, positions, key_pos
    )
    attend_low = cast_reduced(attended)
    attn_out = apply_projection(attend_low, full_o)
    mid = inputs + mamba_out + attn_out
    normed2, norm2_back = jax.vjp(rms_gain, mid, norm2_gain)
    normed2_low = cast_reduced(normed2)
    gate_pre = apply_projection(normed2_low, full_gate)
    up_pre = apply_projection(normed2_low, full_up)
    hidden_act, act_back = jax.vjp(swish_product, gate_pre, up_pre)
    hidden_low = cast_reduced(hidden_act)
    ffn_out = apply_projection(hidden_low, full_down)
    out_hidden = (mid + ffn_out).astype(jnp.bfloat16)
    (
        back_z,
        back_xbc,
        back_dt,
        back_out,
        back_q,
        back_k,
        back_v,
        back_o,
        back_gate,
        back_up,
        back_down,
    ) = (
        lax.all_gather(w_z, ("fsdp", "seq"), axis=0, tiled=True),
        lax.all_gather(w_xbc, ("fsdp", "seq"), axis=0, tiled=True),
        lax.all_gather(w_dt, ("fsdp", "seq"), axis=0, tiled=True),
        lax.all_gather(w_ssm_out, ("fsdp", "seq"), axis=1, tiled=True),
        lax.all_gather(w_q, ("fsdp", "seq"), axis=0, tiled=True),
        lax.all_gather(key_weight, ("fsdp", "seq"), axis=0, tiled=True),
        lax.all_gather(value_weight, ("fsdp", "seq"), axis=0, tiled=True),
        lax.all_gather(w_o, ("fsdp", "seq"), axis=1, tiled=True),
        lax.all_gather(w_gate, ("fsdp", "seq"), axis=0, tiled=True),
        lax.all_gather(w_up, ("fsdp", "seq"), axis=0, tiled=True),
        lax.all_gather(w_down, ("fsdp", "seq"), axis=1, tiled=True),
    )
    upstream = grad_out.astype(jnp.float32)
    upstream_low = cast_reduced(upstream)
    term_down = weight_term(hidden_low, upstream_low)
    grad_act = project_back(upstream_low, back_down)
    grad_gate, grad_up = act_back(grad_act)
    grad_gate_low = cast_reduced(grad_gate)
    grad_up_low = cast_reduced(grad_up)
    term_gate = weight_term(normed2_low, grad_gate_low)
    term_up = weight_term(normed2_low, grad_up_low)
    grad_normed2 = project_back(grad_gate_low, back_gate) + project_back(grad_up_low, back_up)
    grad_mid_add, grad_gain2 = norm2_back(grad_normed2)
    grad_mid = upstream + grad_mid_add
    grad_mid_low = cast_reduced(grad_mid)
    term_o = weight_term(attend_low, grad_mid_low)
    grad_attend_low = cast_reduced(project_back(grad_mid_low, back_o))
    grad_query, key_gradient_gathered, value_gradient_gathered = attention_backward(
        grad_attend_low, query_low, keys_heads, values_heads, softened, probs_low
    )
    key_gradient_portion, grad_value_part = (
        lax.psum_scatter(
            key_gradient_gathered.reshape(number_of_keys, KEY_VALUE_HEADS * HEAD_SIZE).astype(
                jnp.bfloat16
            ),
            "seq",
            scatter_dimension=0,
            tiled=True,
        ).astype(jnp.float32),
        lax.psum_scatter(
            value_gradient_gathered.reshape(number_of_keys, KEY_VALUE_HEADS * HEAD_SIZE).astype(
                jnp.bfloat16
            ),
            "seq",
            scatter_dimension=0,
            tiled=True,
        ).astype(jnp.float32),
    )
    (grad_query_raw,) = query_back(grad_query)
    (key_gradient_unrotated,) = key_pullback_fn(
        key_gradient_portion.reshape(number_of_rows, KEY_VALUE_HEADS, HEAD_SIZE)
    )
    grad_q_low = cast_reduced(grad_query_raw.reshape(number_of_rows, QUERY_HEADS * HEAD_SIZE))
    key_gradient_reduced = cast_reduced(
        key_gradient_unrotated.reshape(number_of_rows, KEY_VALUE_HEADS * HEAD_SIZE)
    )
    grad_v_low = cast_reduced(grad_value_part)
    term_out = weight_term(ssm_low, grad_mid_low)
    grad_ssm = project_back(grad_mid_low, back_out)
    grad_y_local, grad_y_extra, grad_values_tail, grad_gate_z, grad_d_skip, grad_ssm_gain = (
        tail_back(grad_ssm)
    )
    grad_c_corr, grad_log_corr, grad_incoming = corr_back(grad_y_extra)
    prefix_back, later_grad = entering(
        (decay_total, grad_incoming),
        "seq",
        link_states,
        (jnp.ones_like(decay_total), jnp.zeros_like(grad_incoming)),
    )
    grad_total_log = jnp.sum(later_grad * incoming, axis=(1, 2)) * decay_total
    grad_values_ssd, grad_b, grad_c_ssd, grad_step, grad_log_ssd = ssd_back(
        (grad_y_local, later_grad, grad_total_log)
    )
    grad_ext, grad_conv_w, grad_conv_b, grad_dt_raw, grad_dt_bias, grad_a_log = conv_back(
        (
            grad_values_tail + grad_values_ssd,
            grad_b,
            grad_c_corr + grad_c_ssd,
            grad_step,
            grad_log_corr + grad_log_ssd,
        )
    )
    rim_back = from_behind(grad_ext[: KCONV - 1], "seq", -1)
    grad_conv_own = grad_ext[KCONV - 1 :]
    split_at = number_of_rows - (KCONV - 1)
    grad_conv_in = jnp.concatenate(
        [grad_conv_own[:split_at], grad_conv_own[split_at:] + rim_back], axis=0
    )
    grad_xbc_low = cast_reduced(grad_conv_in)
    grad_dt_low = cast_reduced(grad_dt_raw)
    grad_z_low = cast_reduced(grad_gate_z)
    term_z = weight_term(first_normed_reduced, grad_z_low)
    term_xbc = weight_term(first_normed_reduced, grad_xbc_low)
    term_dt = weight_term(first_normed_reduced, grad_dt_low)
    term_q = weight_term(first_normed_reduced, grad_q_low)
    term_k = weight_term(first_normed_reduced, key_gradient_reduced)
    term_v = weight_term(first_normed_reduced, grad_v_low)
    grad_normed1 = (
        project_back(grad_z_low, back_z)
        + project_back(grad_xbc_low, back_xbc)
        + project_back(grad_dt_low, back_dt)
        + project_back(grad_q_low, back_q)
        + project_back(key_gradient_reduced, back_k)
        + project_back(grad_v_low, back_v)
    )
    grad_inputs_add, grad_gain1 = norm1_back(grad_normed1)
    grad_hidden = grad_mid + grad_inputs_add
    (
        shard_z,
        shard_xbc,
        shard_dt,
        shard_out,
        shard_q,
        shard_k,
        shard_v,
        shard_o,
        shard_gate,
        shard_up,
        shard_down,
    ) = (
        lax.psum_scatter(term_z, ("fsdp", "seq"), scatter_dimension=0, tiled=True),
        lax.psum_scatter(term_xbc, ("fsdp", "seq"), scatter_dimension=0, tiled=True),
        lax.psum_scatter(term_dt, ("fsdp", "seq"), scatter_dimension=0, tiled=True),
        lax.psum_scatter(term_out, ("fsdp", "seq"), scatter_dimension=1, tiled=True),
        lax.psum_scatter(term_q, ("fsdp", "seq"), scatter_dimension=0, tiled=True),
        lax.psum_scatter(term_k, ("fsdp", "seq"), scatter_dimension=0, tiled=True),
        lax.psum_scatter(term_v, ("fsdp", "seq"), scatter_dimension=0, tiled=True),
        lax.psum_scatter(term_o, ("fsdp", "seq"), scatter_dimension=1, tiled=True),
        lax.psum_scatter(term_gate, ("fsdp", "seq"), scatter_dimension=0, tiled=True),
        lax.psum_scatter(term_up, ("fsdp", "seq"), scatter_dimension=0, tiled=True),
        lax.psum_scatter(term_down, ("fsdp", "seq"), scatter_dimension=1, tiled=True),
    )
    (
        total_z,
        total_xbc,
        total_dt,
        total_out,
        total_q,
        total_k,
        total_v,
        total_o,
        total_gate,
        total_up,
        total_down,
    ) = (
        lax.psum(shard_z.astype(jnp.bfloat16), "rep").astype(jnp.float32),
        lax.psum(shard_xbc.astype(jnp.bfloat16), "rep").astype(jnp.float32),
        lax.psum(shard_dt.astype(jnp.bfloat16), "rep").astype(jnp.float32),
        lax.psum(shard_out.astype(jnp.bfloat16), "rep").astype(jnp.float32),
        lax.psum(shard_q.astype(jnp.bfloat16), "rep").astype(jnp.float32),
        lax.psum(shard_k.astype(jnp.bfloat16), "rep").astype(jnp.float32),
        lax.psum(shard_v.astype(jnp.bfloat16), "rep").astype(jnp.float32),
        lax.psum(shard_o.astype(jnp.bfloat16), "rep").astype(jnp.float32),
        lax.psum(shard_gate.astype(jnp.bfloat16), "rep").astype(jnp.float32),
        lax.psum(shard_up.astype(jnp.bfloat16), "rep").astype(jnp.float32),
        lax.psum(shard_down.astype(jnp.bfloat16), "rep").astype(jnp.float32),
    )
    (
        sum_gain1,
        sum_conv_w,
        sum_conv_b,
        sum_dt_bias,
        sum_a_log,
        sum_d_skip,
        sum_ssm_gain,
        sum_gain2,
    ) = lax.psum(
        (
            grad_gain1,
            grad_conv_w,
            grad_conv_b,
            grad_dt_bias,
            grad_a_log,
            grad_d_skip,
            grad_ssm_gain,
            grad_gain2,
        ),
        ("rep", "fsdp", "seq"),
    )
    return (
        out_hidden,
        grad_hidden,
        sum_gain1,
        total_z,
        total_xbc,
        total_dt,
        sum_conv_w,
        sum_conv_b,
        sum_dt_bias,
        sum_a_log,
        sum_d_skip,
        sum_ssm_gain,
        total_out,
        total_q,
        total_k,
        total_v,
        total_o,
        sum_gain2,
        total_gate,
        total_up,
        total_down,
    )


def solution(mesh):
    placed = (
        P(("rep", "fsdp", "seq"), None),
        P(),
        P(("fsdp", "seq"), None),
        P(("fsdp", "seq"), None),
        P(("fsdp", "seq"), None),
        P(),
        P(),
        P(),
        P(),
        P(),
        P(),
        P(None, ("fsdp", "seq")),
        P(("fsdp", "seq"), None),
        P(("fsdp", "seq"), None),
        P(("fsdp", "seq"), None),
        P(None, ("fsdp", "seq")),
        P(),
        P(("fsdp", "seq"), None),
        P(("fsdp", "seq"), None),
        P(None, ("fsdp", "seq")),
        P(("rep", "fsdp", "seq"), None),
    )
    return jax.shard_map(
        body,
        mesh=mesh,
        in_specs=placed,
        out_specs=(
            P(("rep", "fsdp", "seq"), None),
            P(("rep", "fsdp", "seq"), None),
            P(),
            P(("fsdp", "seq"), None),
            P(("fsdp", "seq"), None),
            P(("fsdp", "seq"), None),
            P(),
            P(),
            P(),
            P(),
            P(),
            P(),
            P(None, ("fsdp", "seq")),
            P(("fsdp", "seq"), None),
            P(("fsdp", "seq"), None),
            P(("fsdp", "seq"), None),
            P(None, ("fsdp", "seq")),
            P(),
            P(("fsdp", "seq"), None),
            P(("fsdp", "seq"), None),
            P(None, ("fsdp", "seq")),
        ),
        check_vma=False,
    )
```

profile of v0, /device:TPU:0, one launch (start us, length us, event | category | flops | bytes accessed | tf_op | source)
XLA Modules:
  0.0 1383.4 jit_solution(7612275496334096297)
XLA Ops:
  14.5 14.4 %all_gather.68 = bf16[1024,24]{0,1:T(8,128)(2,1)S(1)} all-gather(bf16[128,24]{0,1:T(8,128)(2,1)S(1)} %copy-done.116), channel_id=1, replica_groups=mesh['rep'=4,'fsdp'=4,'seq'=2] {'fsdp','seq'}, dimensions={0}, use_global_device_ids=true | all-gather | bytes 55296 | tf_op jit(solution)/shard_map/all_gather | solution.py:275
  39.5 15.0 %all_gather.77 = bf16[1024,128]{1,0:T(8,128)(2,1)S(1)} all-gather(bf16[128,128]{1,0:T(8,128)(2,1)S(1)} %copy-done.99), channel_id=1, replica_groups=mesh['rep'=4,'fsdp'=4,'seq'=2] {'fsdp','seq'}, dimensions={0}, use_global_device_ids=true | all-gather | bytes 294912 | tf_op jit(solution)/shard_map/all_gather | solution.py:278
  59.2 15.1 %all_gather.75 = bf16[1024,128]{1,0:T(8,128)(2,1)S(1)} all-gather(bf16[128,128]{1,0:T(8,128)(2,1)S(1)} %copy-done.100), channel_id=1, replica_groups=mesh['rep'=4,'fsdp'=4,'seq'=2] {'fsdp','seq'}, dimensions={0}, use_global_device_ids=true | all-gather | bytes 294912 | tf_op jit(solution)/shard_map/all_gather | solution.py:279
  80.6 10.7 fusion.200
  126.6 136.2 %while.73 = (s32[]{:T(128)}, f32[24,64,128]{2,1,0:T(8,128)S(1)}, f32[4,128,24,64]{1,0,3,2:T(4,128)}, f32[4,24,64,128]{3,2,1,0:T(8,128)}, f32[4,128,24]{2,1,0:T(8...) while((s32[]{:T(128)}, f32[24,64,128]{2,1,0:T(8,128)S(1)}, ...), condition=%wide.region_3.4_spmd.clone.clone, body=%wide.region_1.3_spmd.clone.clone.sunk | while | flops 935070720 | bytes 10121433 | solution.py:161
  137.2 20.1 %dynamic_update_slice.84 = f32[4,128,24,64]{1,0,3,2:T(4,128)} dynamic-update-slice(f32[4,128,24,64]{1,0,3,2:T(4,128)} %get-tuple-element.1245, f32[1,128,24,64]{1,0,3,2:T(1,128)S(1)} %bitcast.468, s32[]{:T(128)} %get-tuple-element.1243, s32[]{:T(128)} %constant.191.clone.1..sunk.2, s32[]{:T(128)} %constant.191.clone.1..sunk.2, s32[]{:T(128)} %constant.191.clone.1..sunk.2) | dynamic-update-slice | bytes 1572868 | tf_op jit(solution)/shard_map/jvp()/while/body/jit(dynamic_update_index_in_dim)/dynamic_update_slice | solution.py:161
  171.1 20.1 %dynamic_update_slice.84 = f32[4,128,24,64]{1,0,3,2:T(4,128)} dynamic-update-slice(f32[4,128,24,64]{1,0,3,2:T(4,128)} %get-tuple-element.1245, f32[1,128,24,64]{1,0,3,2:T(1,128)S(1)} %bitcast.468, s32[]{:T(128)} %get-tuple-element.1243, s32[]{:T(128)} %constant.191.clone.1..sunk.2, s32[]{:T(128)} %constant.191.clone.1..sunk.2, s32[]{:T(128)} %constant.191.clone.1..sunk.2) | dynamic-update-slice | bytes 1572868 | tf_op jit(solution)/shard_map/jvp()/while/body/jit(dynamic_update_index_in_dim)/dynamic_update_slice | solution.py:161
  205.2 20.1 %dynamic_update_slice.84 = f32[4,128,24,64]{1,0,3,2:T(4,128)} dynamic-update-slice(f32[4,128,24,64]{1,0,3,2:T(4,128)} %get-tuple-element.1245, f32[1,128,24,64]{1,0,3,2:T(1,128)S(1)} %bitcast.468, s32[]{:T(128)} %get-tuple-element.1243, s32[]{:T(128)} %constant.191.clone.1..sunk.2, s32[]{:T(128)} %constant.191.clone.1..sunk.2, s32[]{:T(128)} %constant.191.clone.1..sunk.2) | dynamic-update-slice | bytes 1572868 | tf_op jit(solution)/shard_map/jvp()/while/body/jit(dynamic_update_index_in_dim)/dynamic_update_slice | solution.py:161
  239.3 20.2 %dynamic_update_slice.84 = f32[4,128,24,64]{1,0,3,2:T(4,128)} dynamic-update-slice(f32[4,128,24,64]{1,0,3,2:T(4,128)} %get-tuple-element.1245, f32[1,128,24,64]{1,0,3,2:T(1,128)S(1)} %bitcast.468, s32[]{:T(128)} %get-tuple-element.1243, s32[]{:T(128)} %constant.191.clone.1..sunk.2, s32[]{:T(128)} %constant.191.clone.1..sunk.2, s32[]{:T(128)} %constant.191.clone.1..sunk.2) | dynamic-update-slice | bytes 1572868 | tf_op jit(solution)/shard_map/jvp()/while/body/jit(dynamic_update_index_in_dim)/dynamic_update_slice | solution.py:161
  313.7 13.2 all-gather.26.cloned.1.call-done
  364.2 11.1 fusion.91
  375.4 9.3 fusion.141
  404.0 127.3 %while.71 = (s32[]{:T(128)}, f32[24,64,128]{2,1,0:T(8,128)S(1)}, f32[4,128,24,64]{1,3,2,0:T(8,128)}, f32[4,128,128]{2,1,0:T(8,128)}, f32[4,128,128]{2,1,0:T(8,12...) while((s32[]{:T(128)}, f32[24,64,128]{2,1,0:T(8,128)S(1)}, ...), condition=%wide.region_27.28_spmd, body=%wide.region_17.27_spmd.sunk | while | flops 2200690688 | bytes 22513312 | solution.py:161
  531.3 11.7 fusion.93
  668.2 30.5 %reduce-scatter.26.cloned.1.call-done = f32[128,512]{1,0:T(8,128)} async-done(((f32[1024,512]{1,0:T(8,128)}), f32[128,512]{1,0:T(8,128)}) %reduce-scatter.26.cloned.1.call-update) | async-done | bytes 262160 | tf_op jit(solution)/shard_map/reduce_scatter | solution.py:482
  700.4 35.1 %reduce-scatter.32.cloned.1.call-done = f32[512,128]{1,0:T(8,128)} async-done(((f32[512,1024]{1,0:T(8,128)}), f32[512,128]{1,0:T(8,128)}) %reduce-scatter.32.cloned.1.call-update) | async-done | bytes 262160 | tf_op jit(solution)/shard_map/reduce_scatter | solution.py:485
  737.1 69.3 %reduce-scatter.24.cloned.1.call-done = f32[1536,128]{1,0:T(8,128)} async-done(((f32[1536,1024]{1,0:T(8,128)}), f32[1536,128]{1,0:T(8,128)}) %reduce-scatter.24.cloned.1.call-update) | async-done | bytes 786448 | tf_op jit(solution)/shard_map/reduce_scatter | solution.py:481
  808.3 68.5 %reduce-scatter.18.cloned.1.call-done = f32[128,1536]{1,0:T(8,128)} async-done(((f32[1024,1536]{1,0:T(8,128)}), f32[128,1536]{1,0:T(8,128)}) %reduce-scatter.18.cloned.1.call-update) | async-done | bytes 786448 | tf_op jit(solution)/shard_map/reduce_scatter | solution.py:478
  878.7 78.5 %reduce-scatter.20.cloned.1.call-done = f32[128,1792]{1,0:T(8,128)} async-done(((f32[1024,1792]{1,0:T(8,128)}), f32[128,1792]{1,0:T(8,128)}) %reduce-scatter.20.cloned.1.call-update) | async-done | bytes 917520 | tf_op jit(solution)/shard_map/reduce_scatter | solution.py:479
  959.1 88.4 %reduce-scatter.34.cloned.1.call-done = f32[128,2048]{1,0:T(8,128)} async-done(((f32[1024,2048]{1,0:T(8,128)}), f32[128,2048]{1,0:T(8,128)}) %reduce-scatter.34.cloned.1.call-update) | async-done | bytes 1048592 | tf_op jit(solution)/shard_map/reduce_scatter | solution.py:486
  1049.6 88.1 %reduce-scatter.36.cloned.1.call-done = f32[128,2048]{1,0:T(8,128)} async-done(((f32[1024,2048]{1,0:T(8,128)}), f32[128,2048]{1,0:T(8,128)}) %reduce-scatter.36.cloned.1.call-update) | async-done | bytes 1048592 | tf_op jit(solution)/shard_map/reduce_scatter | solution.py:487
  1139.9 88.3 %reduce-scatter.38.cloned.1.call-done = f32[2048,128]{1,0:T(8,128)} async-done(((f32[2048,1024]{1,0:T(8,128)}), f32[2048,128]{1,0:T(8,128)}) %reduce-scatter.38.cloned.1.call-update) | async-done | bytes 1048592 | tf_op jit(solution)/shard_map/reduce_scatter | solution.py:488
  1243.3 39.4 %all-reduce.17 = (f32[1024]{0:T(1024)}, f32[4,1792]{1,0:T(4,128)}, f32[1792]{0:T(1024)}, f32[24]{0:T(128)}, f32[24]{0:T(128)}, /*index=5*/f32[24]{0:T(128)}, f32[1536]{0:T(1024)}, f32[1024]{0:T(1024)}) all-reduce(f32[1024]{0:T(1024)S(1)} %get-tuple-element.807, ...), channel_id=1, replica_groups=mesh['rep'=4,'fsdp'=4,'seq'=2] {'rep','fsdp','seq'}, use_global_device_ids=true, to_apply=%region_37.38 | all-reduce | flops 12616 | bytes 100928 | tf_op jit(solution)/shard_map/psum | solution.py:524
  1291.8 75.1 %all-reduce.25.cloned.1.call-done = (bf16[128,1536]{1,0:T(8,128)(2,1)}, bf16[128,1792]{1,0:T(8,128)(2,1)}, bf16[1536,128]{1,0:T(8,128)(2,1)}, bf16[128,512]{1,0:...) async-done(((bf16[128,1536]{1,0:T(8,128)(2,1)}, bf16[128,1792]{1,0:T(8,128)(2,1)}, ...) | async-done | bytes 3080208 | tf_op jit(solution)/shard_map/psum | solution.py:503
  (726 shorter events, 524.2 us)
Async XLA Ops:
  7.2 71.1 %all-gather.18.cloned.1.call-start = ((), (), s32[]{:S(2)}) async-start(), calls=%async_computation.16 | async-start | bytes 1179648 | tf_op jit(solution)/shard_map/all_gather | solution.py:277
  8.0 83.4 %all-gather.12.cloned.1.call-start = ((), (), s32[]{:S(2)}) async-start(), calls=%async_computation.13 | async-start | bytes 4128768 | tf_op jit(solution)/shard_map/all_gather | solution.py:274
  8.7 273.1 %all-gather.14.cloned.1.call-start = ((), (), s32[]{:S(2)}) async-start(), calls=%async_computation.14 | async-start | bytes 3538944 | tf_op jit(solution)/shard_map/all_gather | solution.py:273
  9.5 280.1 %all-gather.16.cloned.1.call-start = ((), (), s32[]{:S(2)}) async-start(), calls=%async_computation.15 | async-start | bytes 3538944 | tf_op jit(solution)/shard_map/all_gather | solution.py:276
  10.1 285.6 %all-gather.20.cloned.1.call-start = ((), (), s32[]{:S(2)}) async-start(), calls=%async_computation.17 | async-start | bytes 1179648 | tf_op jit(solution)/shard_map/all_gather | solution.py:280
  10.6 288.4 %all-gather.22.cloned.1.call-start = ((), (), s32[]{:S(2)}) async-start(), calls=%async_computation.18 | async-start | bytes 4718592 | tf_op jit(solution)/shard_map/all_gather | solution.py:281
  11.2 295.6 %all-gather.24.cloned.1.call-start = ((), (), s32[]{:S(2)}) async-start(), calls=%async_computation.19 | async-start | bytes 4718592 | tf_op jit(solution)/shard_map/all_gather | solution.py:282
  12.0 314.9 %all-gather.26.cloned.1.call-start = ((), (), s32[]{:S(2)}) async-start(), calls=%async_computation.20 | async-start | bytes 4718592 | tf_op jit(solution)/shard_map/all_gather | solution.py:283
  12.7 541.1 %reduce-scatter.14.cloned.1.call-start = ((), (), s32[]{:S(2)}) async-start(), calls=%async_computation.21 | async-start | bytes 393216 | tf_op jit(solution)/shard_map/reduce_scatter | solution.py:389
  95.5 10.7 collective-permute-start
  546.8 17.6 %reduce-scatter.16.cloned.1.call-start = ((), (), s32[]{:S(2)}) async-start(), calls=%async_computation.22 | async-start | bytes 393216 | tf_op jit(solution)/shard_map/reduce_scatter | solution.py:397
  552.3 111.6 %reduce-scatter.22.cloned.1.call-start = ((), (), s32[]{:S(2)}) async-start(), calls=%async_computation.25 | async-start | bytes 110592 | tf_op jit(solution)/shard_map/reduce_scatter | solution.py:480
  553.8 111.4 %reduce-scatter.28.cloned.1.call-start = ((), (), s32[]{:S(2)}) async-start(), calls=%async_computation.28 | async-start | bytes 589824 | tf_op jit(solution)/shard_map/reduce_scatter | solution.py:483
  556.2 110.4 %reduce-scatter.30.cloned.1.call-start = ((), (), s32[]{:S(2)}) async-start(), calls=%async_computation.29 | async-start | bytes 589824 | tf_op jit(solution)/shard_map/reduce_scatter | solution.py:484
  566.6 132.2 %reduce-scatter.26.cloned.1.call-start = ((), (), s32[]{:S(2)}) async-start(), calls=%async_computation.27 | async-start | bytes 2359296 | tf_op jit(solution)/shard_map/reduce_scatter | solution.py:482
  574.0 161.4 %reduce-scatter.32.cloned.1.call-start = ((), (), s32[]{:S(2)}) async-start(), calls=%async_computation.30 | async-start | bytes 2359296 | tf_op jit(solution)/shard_map/reduce_scatter | solution.py:485
  577.2 229.1 %reduce-scatter.24.cloned.1.call-start = ((), (), s32[]{:S(2)}) async-start(), calls=%async_computation.26 | async-start | bytes 7077888 | tf_op jit(solution)/shard_map/reduce_scatter | solution.py:481
  583.7 293.0 %reduce-scatter.18.cloned.1.call-start = ((), (), s32[]{:S(2)}) async-start(), calls=%async_computation.23 | async-start | bytes 7077888 | tf_op jit(solution)/shard_map/reduce_scatter | solution.py:478
  589.7 367.5 %reduce-scatter.20.cloned.1.call-start = ((), (), s32[]{:S(2)}) async-start(), calls=%async_computation.24 | async-start | bytes 8257536 | tf_op jit(solution)/shard_map/reduce_scatter | solution.py:479
  631.7 415.9 %reduce-scatter.34.cloned.1.call-start = ((), (), s32[]{:S(2)}) async-start(), calls=%async_computation.31 | async-start | bytes 9437184 | tf_op jit(solution)/shard_map/reduce_scatter | solution.py:486
  640.2 497.6 %reduce-scatter.36.cloned.1.call-start = ((), (), s32[]{:S(2)}) async-start(), calls=%async_computation.32 | async-start | bytes 9437184 | tf_op jit(solution)/shard_map/reduce_scatter | solution.py:487
  647.5 580.6 %reduce-scatter.38.cloned.1.call-start = ((), (), s32[]{:S(2)}) async-start(), calls=%async_computation.33 | async-start | bytes 9437184 | tf_op jit(solution)/shard_map/reduce_scatter | solution.py:488
  656.0 631.7 %all-reduce.23.cloned.1.call-start = ((), (), s32[]{:S(2)}) async-start(), calls=%async_computation.34 | async-start | bytes 143360 | tf_op jit(solution)/shard_map/psum | solution.py:505
  668.1 698.8 %all-reduce.25.cloned.1.call-start = ((), (), s32[]{:S(2)}) async-start(), calls=%async_computation.35 | async-start | bytes 6160384 | tf_op jit(solution)/shard_map/psum | solution.py:503
  (151 other events, 2250.9 us)
Sparse Core Ops, SparseCore 0:
  9.7 25.0 all-gather.17
  36.4 45.5 all-gather.11
  83.6 37.1 all-gather.13
  122.2 38.0 all-gather.15
  161.8 22.1 all-gather.19
  185.5 45.7 all-gather.21
  232.9 45.8 all-gather.23
  280.4 46.5 all-gather.25
  546.9 5.8 reduce-scatter.13
  555.5 8.8 reduce-scatter.15
  567.2 31.3 reduce-scatter.21
  601.4 29.0 reduce-scatter.27
  633.3 29.1 reduce-scatter.29
  664.7 33.9 reduce-scatter.25
  701.0 34.4 reduce-scatter.31
  737.7 68.5 reduce-scatter.23
  808.6 68.1 reduce-scatter.17
  879.0 78.0 reduce-scatter.19
  959.5 87.9 reduce-scatter.33
  1049.8 87.9 reduce-scatter.35
  1140.2 87.9 reduce-scatter.37
  1232.8 39.2 all-reduce.22
  1277.7 89.1 all-reduce.24
where the time goes:
time: 1400 us; the launch traced here: 1380 us
  waiting for transfers between devices  649 us (46%)
  matrix products  307 us (22%)
  local copies, waits for them, and re-layouts  198 us (14%)
  other arithmetic  112 us (8%)
  blocking collectives  95.5 us (7%)
  between operations  16.5 us (1%)
    reduce_scatter x1, waiting for transfers between devices, body(): lax.psum_scatter(term_gate, ('fsdp', 'seq'), scatter_dimension=0, tiled=T...  88.4 us
    reduce_scatter x1, waiting for transfers between devices, body(): lax.psum_scatter(term_down, ('fsdp', 'seq'), scatter_dimension=1, tiled=T...  88.3 us
    reduce_scatter x1, waiting for transfers between devices, body(): lax.psum_scatter(term_up, ('fsdp', 'seq'), scatter_dimension=0, tiled=True)  88.1 us
    dynamic_update_slice x8, local copies, waits for them, and re-layouts, ssd_local(): final_state, outputs = lax.scan(jax.checkpoint(ssd_block), initial, blocks)  83.1 us
    reduce_scatter x1, waiting for transfers between devices, body(): lax.psum_scatter(term_xbc, ('fsdp', 'seq'), scatter_dimension=0, tiled=True)  78.5 us
    psum x1, waiting for transfers between devices, body(): lax.psum(shard_z.astype(jnp.bfloat16), 'rep').astype(jnp.float32)  75.1 us
    reduce_scatter x1, waiting for transfers between devices, body(): lax.psum_scatter(term_out, ('fsdp', 'seq'), scatter_dimension=1, tiled=True)  69.3 us
    reduce_scatter x1, waiting for transfers between devices, body(): lax.psum_scatter(term_z, ('fsdp', 'seq'), scatter_dimension=0, tiled=True)  68.5 us
  transfers between devices with their start and end apart: 25, of which 11 were waited for; matrix products, arithmetic and copies ran while one was open for 27% of the time, Pallas kernels for 0%

commit v1 on v0

v1 whole, which is shorter than its diff:
```python
import functools

import jax
import jax.numpy as jnp
from jax import lax
from jax.experimental import pallas as pl
from jax.experimental.pallas import tpu as pltpu
from jax.sharding import PartitionSpec as P

NH_SSM = 24
HP = 64
NS = 128
KCONV = 4
QUERY_HEADS = 8
KEY_VALUE_HEADS = 2
HEAD_SIZE = 64
BLOCK = 128
INNER = NH_SSM * HP
CONV = INNER + 2 * NS
LANES = 128
PAIRS = NH_SSM // 2

HIGH = lax.Precision.HIGHEST
EPS = 1e-06
ROPE_BASE = 10000.0
SCALE = HEAD_SIZE ** (-0.5)
LOW = jnp.bfloat16
F32 = jnp.float32


def mm(a, b):
    return jnp.dot(a, b, preferred_element_type=F32)


def mm_nt(a, b):
    return lax.dot_general(a, b, (((1,), (1,)), ((), ())), preferred_element_type=F32)


def mm_tn(a, b):
    return lax.dot_general(a, b, (((0,), (0,)), ((), ())), preferred_element_type=F32)


def halves(v):
    top = v.astype(LOW)
    return top, (v - top.astype(F32)).astype(LOW)


def spread(v, heads):
    top, rest = halves(v)
    return mm(top, heads) + mm(rest, heads)


def gather_heads(v, heads):
    top, rest = halves(v)
    return mm_nt(top, heads) + mm_nt(rest, heads)


def lane_halves(shape):
    lane = lax.broadcasted_iota(jnp.int32, shape, len(shape) - 1)
    return lane % LANES < HP


def stacked(pair, left):
    zero = jnp.zeros_like(pair)
    return jnp.concatenate([jnp.where(left, pair, zero), jnp.where(left, zero, pair)], axis=0)


def states_kernel(conv_ref, halo_ref, taps_ref, step_ref, run_ref, heads_ref, pre_ref, end_ref, ext):
    block = pl.program_id(0)

    @pl.when(block == 0)
    def _():
        ext[0:8, :] = halo_ref[...]
        end_ref[...] = jnp.zeros_like(end_ref)

    @pl.when(block > 0)
    def _():
        ext[0:8, :] = ext[BLOCK : BLOCK + 8, :]

    ext[8 : BLOCK + 8, :] = conv_ref[...].astype(F32)
    pre = taps_ref[KCONV : KCONV + 1, :] + jnp.zeros((BLOCK, CONV), F32)
    for j in range(KCONV):
        pre = pre + taps_ref[j : j + 1, :] * ext[5 + j : 5 + j + BLOCK, :]
    pre_ref[...] = pre
    heads = heads_ref[...]
    run = run_ref[...]
    last = run[BLOCK - 1 : BLOCK, :]
    tail = jnp.exp(last - run) * step_ref[...]
    wide = spread(jnp.concatenate([tail, jnp.broadcast_to(jnp.exp(last), (8, LANES))], axis=0), heads)
    inner = pre[:, :INNER]
    x = inner * jax.nn.sigmoid(inner)
    bp = pre[:, INNER : INNER + NS]
    b_low = (bp * jax.nn.sigmoid(bp)).T.astype(LOW)
    weighted = (x * wide[:BLOCK]).astype(LOW)
    end_ref[...] = end_ref[...] * wide[BLOCK : BLOCK + 1] + mm(b_low, weighted)


def mixer_kernel(
    pre_ref, step_ref, run_ref, runt_ref, start_ref, z_ref, gain_ref, skip_ref, heads_ref,
    out_ref, y_ref, sin_ref, sout_ref, state,
):
    block = pl.program_id(0)

    @pl.when(block == 0)
    def _():
        state[...] = start_ref[...]

    heads = heads_ref[...]
    run = run_ref[...]
    runt = runt_ref[...]
    step = step_ref[...]
    pre = pre_ref[...]
    act = pre * jax.nn.sigmoid(pre)
    x = act[:, :INNER]
    b = act[:, INNER : INNER + NS]
    c_low = act[:, INNER + NS :].astype(LOW)
    last = run[BLOCK - 1 : BLOCK, :]
    wide = spread(
        jnp.concatenate(
            [
                step,
                jnp.exp(run),
                jnp.exp(last - run) * step,
                jnp.broadcast_to(jnp.exp(last), (8, LANES)),
            ],
            axis=0,
        ),
        heads,
    )
    x_step = (x * wide[:BLOCK]).astype(LOW)
    old = state[...]
    old_low = old.astype(LOW)
    sin_ref[0] = old_low
    carried = mm(c_low, old_low) * wide[BLOCK : 2 * BLOCK]
    weighted = (x * wide[2 * BLOCK : 3 * BLOCK]).astype(LOW)
    new = old * wide[3 * BLOCK : 3 * BLOCK + 1] + mm(b.T.astype(LOW), weighted)
    state[...] = new
    sout_ref[0] = new.astype(LOW)
    cb = mm_nt(c_low, b.astype(LOW))
    rows = lax.broadcasted_iota(jnp.int32, (BLOCK, BLOCK), 0)
    cols = lax.broadcasted_iota(jnp.int32, (BLOCK, BLOCK), 1)
    causal = rows >= cols
    left = lane_halves((BLOCK, LANES))
    parts = []
    for p in range(PAIRS):
        mixes = []
        for h in (2 * p, 2 * p + 1):
            gap = run[:, h : h + 1] - runt[h : h + 1, :]
            mixes.append((jnp.exp(jnp.where(causal, gap, -1e30)) * cb).astype(LOW))
        pair = x_step[:, p * LANES : (p + 1) * LANES]
        parts.append(mm(jnp.concatenate(mixes, axis=1), stacked(pair, left)))
    y = jnp.concatenate(parts, axis=1) + carried
    y_ref[...] = y
    z = z_ref[...]
    gated = (y + skip_ref[...] * x) * (z * jax.nn.sigmoid(z))
    inv = lax.rsqrt(jnp.mean(gated * gated, axis=-1, keepdims=True) + EPS)
    out_ref[...] = (gated * inv * gain_ref[...]).astype(LOW)


def gate_back_kernel(
    g_ref, y_ref, pre_ref, z_ref, run_ref, gain_ref, skip_ref, heads_ref,
    gy_ref, gz_ref, sums_ref, first_ref,
):
    @pl.when(pl.program_id(0) == 0)
    def _():
        sums_ref[...] = jnp.zeros_like(sums_ref)
        first_ref[...] = jnp.zeros_like(first_ref)

    heads = heads_ref[...]
    run = run_ref[...]
    last = run[BLOCK - 1 : BLOCK, :]
    wide = spread(
        jnp.concatenate([jnp.exp(run), jnp.broadcast_to(jnp.exp(last), (8, LANES))], axis=0), heads
    )
    inner = pre_ref[:, :INNER]
    x = inner * jax.nn.sigmoid(inner)
    cp = pre_ref[:, INNER + NS :]
    c = cp * jax.nn.sigmoid(cp)
    y = y_ref[...] + skip_ref[...] * x
    z = z_ref[...]
    sig = jax.nn.sigmoid(z)
    swish = z * sig
    gated = y * swish
    inv = lax.rsqrt(jnp.mean(gated * gated, axis=-1, keepdims=True) + EPS)
    g = g_ref[...]
    gg = g * gain_ref[...]
    mean = jnp.mean(gg * gated, axis=-1, keepdims=True)
    g_gated = gg * inv - gated * (inv * inv * inv * mean)
    g_y = g_gated * swish
    gz_ref[...] = (g_gated * y * (sig + swish * (1.0 - sig))).astype(LOW)
    gy_ref[...] = g_y.astype(LOW)
    sums_ref[0:1, :] += jnp.sum(g * gated * inv, axis=0, keepdims=True)
    sums_ref[1:2, :] += jnp.sum(g_y * x, axis=0, keepdims=True)
    scaled = (g_y * wide[:BLOCK]).astype(LOW)
    first_ref[...] = first_ref[...] * wide[BLOCK : BLOCK + 1] + mm(c.T.astype(LOW), scaled)


def mixer_back_kernel(
    gy_ref, y_ref, pre_ref, step_ref, run_ref, runt_ref, later_ref, sin_ref, sout_ref,
    conv_ref, before_ref, halo_ref, taps_ref, skip_ref, heads_ref,
    gconv_ref, gtail_ref, rim_ref, gstep_ref, grun_ref, gend_ref, gtaps_ref,
    grad_state, ext, dext,
):
    index = pl.program_id(0)
    count = pl.num_programs(0)

    @pl.when(index == 0)
    def _():
        grad_state[...] = later_ref[...]
        gtaps_ref[...] = jnp.zeros_like(gtaps_ref)
        dext[BLOCK : BLOCK + 8, :] = jnp.zeros((8, CONV), F32)

    @pl.when(index > 0)
    def _():
        dext[BLOCK : BLOCK + 8, :] = dext[0:8, :]

    heads = heads_ref[...]
    run = run_ref[...]
    runt = runt_ref[...]
    step = step_ref[...]
    pre = pre_ref[...]
    sig = jax.nn.sigmoid(pre)
    act = pre * sig
    x = act[:, :INNER]
    b = act[:, INNER : INNER + NS]
    c = act[:, INNER + NS :]
    b_low = b.astype(LOW)
    c_low = c.astype(LOW)
    last = run[BLOCK - 1 : BLOCK, :]
    wide = spread(
        jnp.concatenate(
            [step, jnp.exp(run), jnp.exp(last - run), jnp.broadcast_to(jnp.exp(last), (8, LANES))],
            axis=0,
        ),
        heads,
    )
    step_wide = wide[:BLOCK]
    tail_wide = wide[2 * BLOCK : 3 * BLOCK]
    gy_low = gy_ref[...]
    gy = gy_low.astype(F32)
    x_step = (x * step_wide).astype(LOW)
    later = grad_state[...]
    later_low = later.astype(LOW)
    scaled = (gy * wide[BLOCK : 2 * BLOCK]).astype(LOW)
    weighted = (x * (step_wide * tail_wide)).astype(LOW)
    grad_b = mm_nt(weighted, later_low)
    grad_c = mm_nt(scaled, sin_ref[0])
    from_state = mm(b_low, later_low) * tail_wide
    grad_state[...] = later * wide[3 * BLOCK : 3 * BLOCK + 1] + mm(c.T.astype(LOW), scaled)
    ends = jnp.sum(later * sout_ref[0].astype(F32), axis=0, keepdims=True)
    gend_ref[0] = gather_heads(jnp.broadcast_to(ends, (8, INNER)), heads)
    cbt = mm_nt(b_low, c_low)
    rows = lax.broadcasted_iota(jnp.int32, (BLOCK, BLOCK), 0)
    cols = lax.broadcasted_iota(jnp.int32, (BLOCK, BLOCK), 1)
    left = lane_halves((BLOCK, LANES))
    parts = []
    grad_cb = jnp.zeros((BLOCK, BLOCK), F32)
    for p in range(PAIRS):
        lanes = slice(p * LANES, (p + 1) * LANES)
        gy_stack = stacked(gy_low[:, lanes], left)
        products = mm_nt(gy_stack, x_step[:, lanes])
        mixes = []
        for k, h in enumerate((2 * p, 2 * p + 1)):
            column = jnp.broadcast_to(run[:, h : h + 1], (BLOCK, BLOCK))
            gap = column - runt[h : h + 1, :]
            decay = jnp.exp(jnp.where(rows >= cols, gap, -1e30))
            grad_cb = grad_cb + products[k * BLOCK : (k + 1) * BLOCK] * decay
            decay_t = jnp.exp(jnp.where(cols >= rows, -gap, -1e30))
            mixes.append((decay_t * cbt).astype(LOW))
        parts.append(mm(jnp.concatenate(mixes, axis=1), gy_stack))
    u = jnp.concatenate(parts, axis=1) + from_state
    both = gather_heads(
        jnp.concatenate([gy * y_ref[...], x * u], axis=0), heads
    )
    gstep_ref[...] = both[BLOCK:]
    grun_ref[...] = both[:BLOCK] - step * both[BLOCK:]
    grad_cb_low = grad_cb.astype(LOW)
    grad_c = grad_c + mm(grad_cb_low, b_low)
    grad_b = grad_b + mm(grad_cb.T.astype(LOW), c_low)
    grad_x = u * step_wide + skip_ref[...] * gy
    dpre = jnp.concatenate([grad_x, grad_b, grad_c], axis=1) * (sig + act * (1.0 - sig))
    dext[0:BLOCK, :] = dpre
    k = count - 1 - index
    ext[0:8, :] = jnp.where(k == 0, halo_ref[...], before_ref[BLOCK - 16 :, :].astype(F32)[8:])
    ext[8 : BLOCK + 8, :] = conv_ref[...].astype(F32)
    total = jnp.zeros((BLOCK, CONV), F32)
    for j in range(KCONV):
        total = total + taps_ref[j : j + 1, :] * dext[KCONV - 1 - j : KCONV - 1 - j + BLOCK, :]
        gtaps_ref[j : j + 1, :] += jnp.sum(dpre * ext[5 + j : 5 + j + BLOCK, :], axis=0, keepdims=True)
    gtaps_ref[KCONV : KCONV + 1, :] += jnp.sum(dpre, axis=0, keepdims=True)
    gconv_ref[...] = total.astype(LOW)

    @pl.when(index == 0)
    def _():
        gtail_ref[...] = total[BLOCK - 8 :, :]

    rim_ref[...] = dpre[0:8, :]


def fixed(shape):
    return pl.BlockSpec(shape, lambda i: (0,) * len(shape))


def params(mib):
    return pltpu.CompilerParams(
        dimension_semantics=("arbitrary",), vmem_limit_bytes=mib * 1024 * 1024
    )


def rows_of(width):
    return pl.BlockSpec((BLOCK, width), lambda i: (i, 0))


def mixer_states(conv_low, halo, taps, step, run, heads):
    rows = conv_low.shape[0]
    return pl.pallas_call(
        states_kernel,
        grid=(rows // BLOCK,),
        in_specs=[rows_of(CONV), fixed((8, CONV)), fixed((8, CONV)), rows_of(LANES), rows_of(LANES),
                  fixed((LANES, INNER))],
        out_specs=[rows_of(CONV), fixed((NS, INNER))],
        out_shape=[jax.ShapeDtypeStruct((rows, CONV), F32), jax.ShapeDtypeStruct((NS, INNER), F32)],
        scratch_shapes=[pltpu.VMEM((BLOCK + 8, CONV), F32)],
        compiler_params=params(40),
        name="mixer_states",
    )(conv_low, halo, taps, step, run, heads)


def mixer_forward(pre, step, run, runt, start, z, gain, skip, heads):
    rows = pre.shape[0]
    count = rows // BLOCK
    state_spec = pl.BlockSpec((1, NS, INNER), lambda i: (i, 0, 0))
    return pl.pallas_call(
        mixer_kernel,
        grid=(count,),
        in_specs=[rows_of(CONV), rows_of(LANES), rows_of(LANES), rows_of(LANES), fixed((NS, INNER)),
                  rows_of(INNER), fixed((1, INNER)), fixed((1, INNER)), fixed((LANES, INNER))],
        out_specs=[rows_of(INNER), rows_of(INNER), state_spec, state_spec],
        out_shape=[
            jax.ShapeDtypeStruct((rows, INNER), LOW),
            jax.ShapeDtypeStruct((rows, INNER), F32),
            jax.ShapeDtypeStruct((count, NS, INNER), LOW),
            jax.ShapeDtypeStruct((count, NS, INNER), LOW),
        ],
        scratch_shapes=[pltpu.VMEM((NS, INNER), F32)],
        compiler_params=params(40),
        name="mixer_forward",
    )(pre, step, run, runt, start, z, gain, skip, heads)


def gate_back(g, y, pre, z, run, gain, skip, heads):
    rows = pre.shape[0]
    count = rows // BLOCK

    def back(width):
        return pl.BlockSpec((BLOCK, width), lambda i: (count - 1 - i, 0))

    return pl.pallas_call(
        gate_back_kernel,
        grid=(count,),
        in_specs=[back(INNER), back(INNER), back(CONV), back(INNER), back(LANES), fixed((1, INNER)),
                  fixed((1, INNER)), fixed((LANES, INNER))],
        out_specs=[back(INNER), back(INNER), fixed((8, INNER)), fixed((NS, INNER))],
        out_shape=[
            jax.ShapeDtypeStruct((rows, INNER), LOW),
            jax.ShapeDtypeStruct((rows, INNER), LOW),
            jax.ShapeDtypeStruct((8, INNER), F32),
            jax.ShapeDtypeStruct((NS, INNER), F32),
        ],
        compiler_params=params(40),
        name="gate_back",
    )(g, y, pre, z, run, gain, skip, heads)


def mixer_back(gy, y, pre, step, run, runt, later, s_in, s_out, conv_low, halo, taps, skip, heads):
    rows = pre.shape[0]
    count = rows // BLOCK

    def back(width):
        return pl.BlockSpec((BLOCK, width), lambda i: (count - 1 - i, 0))

    state_spec = pl.BlockSpec((1, NS, INNER), lambda i: (count - 1 - i, 0, 0))
    before = pl.BlockSpec((BLOCK, CONV), lambda i: (jnp.maximum(count - 2 - i, 0), 0))
    return pl.pallas_call(
        mixer_back_kernel,
        grid=(count,),
        in_specs=[back(INNER), back(INNER), back(CONV), back(LANES), back(LANES), back(LANES),
                  fixed((NS, INNER)), state_spec, state_spec, back(CONV), before, fixed((8, CONV)),
                  fixed((8, CONV)), fixed((1, INNER)), fixed((LANES, INNER))],
        out_specs=[back(CONV), fixed((8, CONV)), fixed((8, CONV)), back(LANES), back(LANES),
                   pl.BlockSpec((1, 8, LANES), lambda i: (count - 1 - i, 0, 0)), fixed((8, CONV))],
        out_shape=[
            jax.ShapeDtypeStruct((rows, CONV), LOW),
            jax.ShapeDtypeStruct((8, CONV), F32),
            jax.ShapeDtypeStruct((8, CONV), F32),
            jax.ShapeDtypeStruct((rows, LANES), F32),
            jax.ShapeDtypeStruct((rows, LANES), F32),
            jax.ShapeDtypeStruct((count, 8, LANES), F32),
            jax.ShapeDtypeStruct((8, CONV), F32),
        ],
        scratch_shapes=[
            pltpu.VMEM((NS, INNER), F32),
            pltpu.VMEM((BLOCK + 8, CONV), F32),
            pltpu.VMEM((BLOCK + 8, CONV), F32),
        ],
        compiler_params=params(48),
        name="mixer_back",
    )(gy, y, pre, step, run, runt, later, s_in, s_out, conv_low, conv_low, halo, taps, skip, heads)


def turned(x, cosine, sine):
    half = HEAD_SIZE // 2
    lane = lax.broadcasted_iota(jnp.int32, x.shape, 1)
    other = jnp.where(
        lane % HEAD_SIZE < half, pltpu.roll(x, LANES - half, axis=1), pltpu.roll(x, half, axis=1)
    )
    return x * cosine + other * sine


def group_keys(value, group, left):
    other = pltpu.roll(value, HEAD_SIZE, axis=1)
    return jnp.where(left == (group == 0), value, other).astype(LOW)


def group_rows(value, group):
    turned_over = value.T
    return jnp.where(group == 0, turned_over[:HEAD_SIZE], turned_over[HEAD_SIZE:]).astype(LOW)


def attend_kernel(first_ref, q_ref, cos_ref, sin_ref, kv_ref, out_ref, q_low_ref, norm_ref):
    keys, rows = kv_ref.shape[0], q_ref.shape[0]
    group = pl.program_id(0) // 2
    left = lane_halves((rows, LANES))
    key_at = lax.broadcasted_iota(jnp.int32, (keys, rows), 0)
    query_at = lax.broadcasted_iota(jnp.int32, (keys, rows), 1) + first_ref[0]
    seen = key_at <= query_at
    q = (turned(q_ref[...], cos_ref[...], sin_ref[...]).astype(LOW) * SCALE).astype(LOW)
    q_low_ref[...] = q
    k = group_keys(kv_ref[:, :LANES].astype(F32), group, lane_halves((keys, LANES)))
    vt = group_rows(kv_ref[:, LANES:].astype(F32), group)
    zero = jnp.zeros_like(q)
    parts = []
    norm_ref[...] = jnp.zeros_like(norm_ref)
    for n in range(2):
        mine = jnp.where(left, q, zero) if n == 0 else jnp.where(left, zero, q)
        scores = jnp.where(seen, mm_nt(k, mine), -1e30)
        peak = jnp.max(scores, axis=0, keepdims=True)
        raised = jnp.exp(scores - peak)
        total = jnp.sum(raised, axis=0, keepdims=True)
        probs = (raised * (1.0 / total)).astype(LOW)
        norm_ref[0, n : n + 1, :] = peak + jnp.log(total)
        parts.append(mm(vt, probs))
    out_ref[...] = jnp.concatenate(parts, axis=0).T.astype(LOW)


def attend_back_kernel(
    first_ref, g_ref, q_ref, cos_ref, sin_ref, kv_ref, norm_ref, gq_ref, gkv_ref
):
    keys, rows = kv_ref.shape[0], q_ref.shape[0]
    step = pl.program_id(0)
    group = step // 2
    left = lane_halves((rows, LANES))
    key_left = lane_halves((keys, LANES))
    key_at = lax.broadcasted_iota(jnp.int32, (keys, rows), 0)
    query_at = lax.broadcasted_iota(jnp.int32, (keys, rows), 1) + first_ref[0]
    seen = key_at <= query_at
    q = q_ref[...]
    g = g_ref[...].astype(LOW)
    k_wide = kv_ref[:, :LANES].astype(F32)
    k = group_keys(k_wide, group, key_left)
    kt = group_rows(k_wide, group)
    v = group_keys(kv_ref[:, LANES:].astype(F32), group, key_left)
    zero = jnp.zeros_like(q)
    parts = []
    gk = jnp.zeros((keys, LANES), F32)
    gv = jnp.zeros((keys, LANES), F32)
    for n in range(2):
        mine = jnp.where(left, q, zero) if n == 0 else jnp.where(left, zero, q)
        grad = jnp.where(left, g, zero) if n == 0 else jnp.where(left, zero, g)
        scores = jnp.where(seen, mm_nt(k, mine), -1e30)
        probs = jnp.exp(scores - norm_ref[0, n : n + 1, :])
        g_probs = mm_nt(v, grad)
        inner = jnp.sum(probs * g_probs, axis=0, keepdims=True)
        g_scores = (probs * (g_probs - inner)).astype(LOW)
        gk = gk + mm(g_scores, mine)
        gv = gv + mm(probs.astype(LOW), grad)
        parts.append(mm(kt, g_scores))
    grad_q = jnp.concatenate(parts, axis=0).T * SCALE
    gq_ref[...] = turned(grad_q, cos_ref[...], -sin_ref[...]).astype(LOW)
    here = key_left == (group == 0)

    @pl.when(step == 0)
    def _():
        gkv_ref[...] = jnp.zeros_like(gkv_ref)

    for n, value in enumerate((gk, gv)):
        both = value + pltpu.roll(value, HEAD_SIZE, axis=1)
        gkv_ref[:, n * LANES : (n + 1) * LANES] += jnp.where(here, both, 0.0)


def attend(first, proj, q_at, cosine, sine, kv):
    rows, keys = proj.shape[0], kv.shape[0]
    count = QUERY_HEADS // 2
    column = pl.BlockSpec((rows, LANES), lambda i: (0, i))
    low = jax.ShapeDtypeStruct((rows, QUERY_HEADS * HEAD_SIZE), LOW)
    return pl.pallas_call(
        attend_kernel,
        grid=(count,),
        in_specs=[
            pl.BlockSpec(memory_space=pltpu.SMEM),
            pl.BlockSpec((rows, LANES), lambda i: (0, q_at // LANES + i)),
            fixed((rows, LANES)),
            fixed((rows, LANES)),
            fixed((keys, 2 * LANES)),
        ],
        out_specs=[column, column, pl.BlockSpec((1, 8, rows), lambda i: (i, 0, 0))],
        out_shape=[low, low, jax.ShapeDtypeStruct((count, 8, rows), F32)],
        compiler_params=params(48),
        name="attend",
    )(first, proj, cosine, sine, kv)


def attend_back(first, g, g_at, q, cosine, sine, kv, norm):
    rows, keys = q.shape[0], kv.shape[0]
    count = QUERY_HEADS // 2
    column = pl.BlockSpec((rows, LANES), lambda i: (0, i))
    return pl.pallas_call(
        attend_back_kernel,
        grid=(count,),
        in_specs=[
            pl.BlockSpec(memory_space=pltpu.SMEM),
            pl.BlockSpec((rows, LANES), lambda i: (0, g_at // LANES + i)),
            column,
            fixed((rows, LANES)),
            fixed((rows, LANES)),
            fixed((keys, 2 * LANES)),
            pl.BlockSpec((1, 8, rows), lambda i: (i, 0, 0)),
        ],
        out_specs=[column, fixed((keys, 2 * LANES))],
        out_shape=[
            jax.ShapeDtypeStruct(q.shape, LOW),
            jax.ShapeDtypeStruct((keys, 2 * LANES), F32),
        ],
        compiler_params=params(48),
        name="attend_back",
    )(first, g, q, cosine, sine, kv, norm)


def trade(value, axis, bit):
    count = lax.axis_size(axis)
    return lax.ppermute(value, axis, [(i, i ^ bit) for i in range(count)])


def shifted(value, axis, by):
    count = lax.axis_size(axis)
    return lax.ppermute(value, axis, [(i, (i + by) % count) for i in range(count)])


def from_behind(value, axis, by):
    count = lax.axis_size(axis)
    pairs = [(i, i + by) for i in range(count) if 0 <= i + by < count]
    return lax.ppermute(value, axis, pairs)


def bits_of(count, flip):
    bits = [1 << k for k in range(count.bit_length() - 1)]
    return bits[::-1] if flip else bits


class Flow:
    def __init__(self, steps):
        self.steps, self.value = steps, None
        self.pending = next(steps)

    def advance(self, arrived):
        try:
            self.pending = self.steps.send(arrived)
        except StopIteration as end:
            self.pending, self.value = [], end.value


def tick(flows, values):
    arrived, values = lax.optimization_barrier(([f.pending for f in flows], values))
    for flow, got in zip(flows, arrived):
        flow.advance(got)
    return values


def sharing(own, split):
    reps = lax.axis_size("rep")
    held = [{0: own[:, :split]}, {0: own[:, split:]}]
    for bits in zip(bits_of(reps, False), bits_of(reps, True)):
        orders = [sorted(h) for h in held]
        sent = [jnp.concatenate([h[b] for b in order], axis=0) for h, order in zip(held, orders)]
        got = yield [trade(v, "rep", bit) for v, bit in zip(sent, bits)]
        for h, order, bit, value in zip(held, orders, bits, got):
            value = value.reshape(len(order), -1, value.shape[1])
            for k, b in enumerate(order):
                h[b ^ bit] = value[k]
    return [[h[b] for b in range(reps)] for h in held]


def gathering(shard, split):
    reps, depth = lax.axis_size("rep"), lax.axis_size("fsdp")
    rep = lax.axis_index("rep")
    unit = shard.shape[0] // reps
    quarters = [lax.dynamic_slice_in_dim(shard, (rep ^ b) * unit, unit, 0) for b in range(reps)]
    far = yield [shifted(quarters[0], "fsdp", s) for s in range(1, depth)]
    shared = yield from sharing(jnp.concatenate(far, axis=0), split)
    sides = []
    for side, columns in zip(shared, (slice(0, split), slice(split, None))):
        parts = [part for b in range(reps) for part in (quarters[b][:, columns], side[b])]
        sides.append(jnp.concatenate(parts, axis=0))
    own = jnp.concatenate(sides, axis=1)
    return [own] + (yield [trade(own, "seq", a) for a in range(1, lax.axis_size("seq"))])


def reducing(left, right, split):
    seqs, reps, depth = lax.axis_size("seq"), lax.axis_size("rep"), lax.axis_size("fsdp")
    part = left.shape[1] // seqs
    sent = [mm_tn(left[:, a * part : (a + 1) * part], right).astype(LOW) for a in range(1, seqs)]
    got = yield [trade(value, "seq", a + 1) for a, value in enumerate(sent)]
    total = mm_tn(left[:, :part], right)
    for value in got:
        total = total + value.astype(F32)
    total = total.reshape(reps, part // reps, right.shape[1])
    held = [{b: total[b, :, :split] for b in range(reps)}, {b: total[b, :, split:] for b in range(reps)}]
    for bits in zip(bits_of(reps, False), bits_of(reps, True)):
        away = [sorted(b for b in h if b & bit) for h, bit in zip(held, bits)]
        sent = [jnp.concatenate([h[b] for b in bs], axis=0).astype(LOW) for h, bs in zip(held, away)]
        got = yield [trade(v, "rep", bit) for v, bit in zip(sent, bits)]
        for n, (h, bs, bit, value) in enumerate(zip(held, away, bits, got)):
            value = value.reshape(len(bs), -1, value.shape[1])
            held[n] = {b: h[b] + value[bs.index(b ^ bit)].astype(F32) for b in h if not b & bit}
    mine = jnp.concatenate([held[0][0], held[1][0]], axis=1).reshape(depth, -1, right.shape[1])
    got = yield [shifted(mine[s].astype(LOW), "fsdp", -s) for s in range(1, depth)]
    total = mine[0]
    for value in got:
        total = total + value.astype(F32)
    return total.astype(LOW)


def completing(own, split):
    left, right = yield from sharing(own, split)
    rep = lax.axis_index("rep")
    sides = []
    for side in (left, right):
        stack = jnp.stack(side)
        ordered = [lax.dynamic_index_in_dim(stack, rep ^ q, 0, False) for q in range(len(side))]
        sides.append(jnp.concatenate(ordered, axis=0))
    return jnp.concatenate(sides, axis=1).astype(F32)


def summing(value):
    for axis in ("seq", "rep", "fsdp"):
        for bit in bits_of(lax.axis_size(axis), False):
            (got,) = yield [trade(value, axis, bit)]
            value = value + got
    return value


def into(x, weight):
    part = x.shape[1] // len(weight)
    return sum(mm(x[:, a * part : (a + 1) * part], w) for a, w in enumerate(weight))


def out_of(pairs):
    count = len(pairs[0][1])
    return jnp.concatenate([sum(mm_nt(g, weight[a]) for g, weight in pairs) for a in range(count)], axis=1)


def rms_back(g, v, gain):
    r = lax.rsqrt(jnp.mean(v * v, axis=-1, keepdims=True) + EPS)
    scaled = g * gain
    mean = jnp.mean(scaled * v, axis=-1, keepdims=True)
    return r * scaled - v * (r * r * r * mean), jnp.sum(g * v * r, axis=0, keepdims=True)


def rms_gain(v, gain):
    return v * lax.rsqrt(jnp.mean(v * v, axis=-1, keepdims=True) + EPS) * gain


def swap_halves(x):
    half = HEAD_SIZE // 2
    pieces = []
    for start in range(0, x.shape[1], HEAD_SIZE):
        pieces += [x[:, start + half : start + HEAD_SIZE], x[:, start : start + half]]
    return jnp.concatenate(pieces, axis=1)


def body(
    hidden_in, norm1_gain, w_z, w_xbc, w_dt, conv_w, conv_b, dt_bias, a_log, d_skip, ssm_gain, w_ssm_out,
    w_q, key_weight, value_weight, w_o, norm2_gain, w_gate, w_up, w_down, grad_out,
):
    rows, width = hidden_in.shape
    seqs, reps, depth = lax.axis_size("seq"), lax.axis_size("rep"), lax.axis_size("fsdp")
    core, rep, deep = lax.axis_index("seq"), lax.axis_index("rep"), lax.axis_index("fsdp")
    shard = w_z.shape[0]
    unit = shard // reps
    blocks = rows // BLOCK

    place = jnp.arange(width, dtype=jnp.int32)
    u, s = place % unit, place // unit % depth
    b, a = place // (unit * depth) % reps, place // (unit * depth * reps)
    source = ((((deep - s) % depth) * seqs + (core ^ a)) * reps + (rep ^ b)) * unit + u
    order = (place[:, None] == source[None, :]).astype(LOW)

    pack_a = jnp.concatenate(
        [w_z, w_q, key_weight, value_weight, w_xbc, jnp.pad(w_dt, ((0, 0), (0, LANES - NH_SSM)))], axis=1
    )
    q_at, k_at, v_at, conv_at, dt_at = INNER, INNER + 512, INNER + 640, INNER + 768, INNER + 768 + CONV
    flow_a = Flow(gathering(pack_a, 2176))
    pack_b = jnp.concatenate([w_ssm_out, w_o], axis=0).T
    pack_c = jnp.concatenate([w_gate, w_up], axis=1)
    pack_d = w_down.T
    gains = jnp.dot(
        jnp.concatenate([norm1_gain[None], norm2_gain[None], jnp.zeros((6, width), F32)], axis=0),
        order.astype(F32), precision=HIGH,
    )
    gain_1, gain_2 = gains[0:1], gains[1:2]
    inputs = mm(hidden_in, order)
    upstream_low = mm(grad_out, order).astype(LOW)
    normed_1 = rms_gain(inputs, gain_1).astype(LOW)
    inputs = inputs.astype(LOW)
    pack_b, pack_c, pack_d, inputs, upstream_low, normed_1, order = tick(
        [flow_a], (pack_b, pack_c, pack_d, inputs, upstream_low, normed_1, order)
    )
    flow_b = Flow(gathering(pack_b, 1024))

    lanes = jnp.arange(LANES, dtype=jnp.int32)
    half = HEAD_SIZE // 2
    frequency = ROPE_BASE ** (-(lanes % half).astype(F32) / half)
    positions = core * rows + jnp.arange(rows, dtype=jnp.int32)
    angles = positions.astype(F32)[:, None] * frequency[None, :]
    cosine = jnp.cos(angles)
    sine = jnp.sin(angles) * jnp.where(lanes % HEAD_SIZE < half, -1.0, 1.0)[None, :]
    heads = (jnp.arange(LANES)[:, None] == jnp.arange(INNER)[None, :] // HP).astype(LOW)
    taps = jnp.concatenate([conv_w, conv_b[None], jnp.zeros((3, CONV), F32)], axis=0)
    skip = jnp.repeat(d_skip, HP)[None, :]
    gain_s = ssm_gain[None, :]
    pack_c, pack_d, cosine, sine, heads, taps, skip = tick(
        [flow_a], (pack_c, pack_d, cosine, sine, heads, taps, skip)
    )
    flow_c = Flow(gathering(pack_c, 2048))
    pack_d = tick([flow_a, flow_b], pack_d)
    normed_1, pack_d = tick([flow_a, flow_b], (normed_1, pack_d))
    full_a = flow_a.value
    flow_d = Flow(gathering(pack_d, 1024))

    proj = into(normed_1, full_a)
    conv_low = proj[:, conv_at:dt_at].astype(LOW)
    dt_raw = proj[:, dt_at:]
    k_raw = proj[:, k_at:v_at]
    k_low = (k_raw * cosine + swap_halves(k_raw) * sine).astype(LOW)
    kv = lax.all_gather(
        jnp.concatenate([k_low, proj[:, v_at:conv_at].astype(LOW)], axis=1), "seq", axis=0, tiled=True
    )
    halo = from_behind(conv_low[rows - 8 :], "seq", 1).astype(F32)
    step = jax.nn.softplus(dt_raw[:, :NH_SSM] + dt_bias[None, :])
    rate = jnp.exp(a_log)[None, :]
    log_decay = -step * rate
    lower = (jnp.arange(BLOCK)[:, None] >= jnp.arange(BLOCK)[None, :]).astype(F32)
    pad = ((0, 0), (0, LANES - NH_SSM))
    step_pad = jnp.pad(step, pad)
    run = jnp.einsum(
        "ts,ksh->kth", lower, jnp.pad(log_decay, pad).reshape(blocks, BLOCK, LANES), precision=HIGH
    )
    runt = jnp.swapaxes(run, 1, 2).reshape(rows, LANES)
    whole_decay = jnp.exp(jnp.sum(run[:, BLOCK - 1, :NH_SSM], axis=0))
    decay_wide = jnp.repeat(whole_decay, HP)[None, :]
    run = run.reshape(rows, LANES)
    pre, end_state = mixer_states(conv_low, halo, taps, step_pad, run, heads)
    kv, pre, end_state, proj = tick([flow_b, flow_c], (kv, pre, end_state, proj))

    incoming = jnp.zeros_like(end_state)
    for _ in range(seqs - 1):
        incoming = from_behind((end_state + decay_wide * incoming).astype(LOW), "seq", 1).astype(F32)
    start = (core * rows).astype(jnp.int32)[None]
    attended, q_low, norms = attend(start, proj, q_at, cosine, sine, kv)
    incoming, attended, proj = tick([flow_b, flow_c], (incoming, attended, proj))
    full_b = flow_b.value

    ssm_low, y, s_in, s_out = mixer_forward(
        pre, step_pad, run, runt, incoming, proj, gain_s, skip, heads
    )
    both = jnp.concatenate([ssm_low, attended], axis=1)
    both, y, s_in, s_out = tick([flow_c, flow_d], (both, y, s_in, s_out))

    mid = inputs.astype(F32) + out_of([(both, full_b)])
    normed_2 = rms_gain(mid, gain_2).astype(LOW)
    mid, normed_2 = tick([flow_c, flow_d], (mid, normed_2))
    full_c = flow_c.value

    gate_up = into(normed_2, full_c)
    hidden = gate_up.shape[1] // 2
    gate_pre, up_pre = gate_up[:, :hidden], gate_up[:, hidden:]
    sig = jax.nn.sigmoid(gate_pre)
    swish = gate_pre * sig
    act = (swish * up_pre).astype(LOW)
    act, gate_up = tick([flow_d], (act, gate_up))
    act, gate_up = tick([flow_d], (act, gate_up))
    full_d = flow_d.value

    sum_d = Flow(reducing(upstream_low, act, 1024))
    gate_pre, up_pre = gate_up[:, :hidden], gate_up[:, hidden:]
    sig = jax.nn.sigmoid(gate_pre)
    swish = gate_pre * sig
    g_act = into(upstream_low, full_d)
    g_gate_up = jnp.concatenate(
        [(g_act * up_pre * (sig + swish * (1.0 - sig))).astype(LOW), (g_act * swish).astype(LOW)], axis=1
    )
    g_gate_up, act = tick([sum_d], (g_gate_up, act))

    sum_c = Flow(reducing(normed_2, g_gate_up, 2048))
    g_n2 = out_of([(g_gate_up, full_c)])
    upstream = upstream_low.astype(F32)
    g_add, g_gain_2 = rms_back(g_n2, mid, gain_2)
    g_mid = upstream + g_add
    g_low = g_mid.astype(LOW)
    g_both = into(g_low, full_b)
    g_low, g_both, g_mid = tick([sum_d, sum_c], (g_low, g_both, g_mid))

    sum_b = Flow(reducing(g_low, both, 1024))
    gy, gz, gate_sums, first_grad = gate_back(g_both, y, pre, proj, run, gain_s, skip, heads)
    later = jnp.zeros_like(first_grad)
    for _ in range(seqs - 1):
        later = from_behind((first_grad + decay_wide * later).astype(LOW), "seq", -1).astype(F32)
    g_q, g_kv = attend_back(start, g_both, INNER, q_low, cosine, sine, kv, norms)
    gy, gz, later, g_q, g_kv = tick([sum_d, sum_c, sum_b], (gy, gz, later, g_q, g_kv))

    own_kv = lax.dynamic_slice_in_dim(g_kv, core * rows, rows, 0)
    for shift in range(1, seqs):
        part = lax.dynamic_slice_in_dim(g_kv, ((core + shift) % seqs) * rows, rows, 0).astype(LOW)
        own_kv = own_kv + shifted(part, "seq", shift).astype(F32)
    g_k = own_kv[:, :LANES]
    g_k_low = (g_k * cosine - swap_halves(g_k) * sine).astype(LOW)
    g_second = jnp.concatenate([gz, g_q, g_k_low, own_kv[:, LANES:].astype(LOW)], axis=1)
    out_perm = (mid + out_of([(act, full_d)])).astype(LOW)
    out_hidden = mm_nt(out_perm, order).astype(LOW)
    g_second, gy, out_hidden = tick([sum_d, sum_c, sum_b], (g_second, gy, out_hidden))

    sum_a1 = Flow(reducing(normed_1, g_second, 1152))
    g_conv, g_tail, rim, g_step, g_run, g_end, g_taps = mixer_back(
        gy, y, pre, step_pad, run, runt, later, s_in, s_out, conv_low, halo, taps, skip, heads
    )
    g_conv, g_tail, rim, g_step, g_run, g_end, g_taps = tick(
        [sum_c, sum_b, sum_a1], (g_conv, g_tail, rim, g_step, g_run, g_end, g_taps)
    )
    rim_back = jnp.concatenate(
        [
            sum(
                conv_w[j][None] * rim[t + KCONV - 1 - j : t + KCONV - j]
                for j in range(KCONV)
                if t + KCONV - 1 - j >= 0
            )
            for t in range(1 - KCONV, 0)
        ],
        axis=0,
    )
    rim_back = from_behind(rim_back, "seq", -1)
    tail = jnp.concatenate([g_tail[: 9 - KCONV], g_tail[9 - KCONV :] + rim_back], axis=0).astype(LOW)
    g_conv = lax.dynamic_update_slice(g_conv, tail, (rows - 8, 0))
    g_log = jnp.einsum("ts,kth->ksh", lower, g_run.reshape(blocks, BLOCK, LANES), precision=HIGH)
    g_log = (g_log + g_end[:, 0:1, :]).reshape(rows, LANES)[:, :NH_SSM]
    g_step = g_step[:, :NH_SSM] - g_log * rate
    g_dt = g_step * jax.nn.sigmoid(dt_raw[:, :NH_SSM] + dt_bias[None, :])
    g_a_log = jnp.sum(g_log * log_decay, axis=0)
    g_dt_bias = jnp.sum(g_dt, axis=0)
    g_first = jnp.concatenate([g_conv, jnp.pad(g_dt, pad).astype(LOW)], axis=1)
    sum_a2 = Flow(reducing(normed_1, g_first, 1024))
    g_n1 = out_of([(g_second, [w[:, :conv_at] for w in full_a]), (g_first, [w[:, conv_at:] for w in full_a])])
    g_n1, g_mid = tick([sum_b, sum_a1, sum_a2], (g_n1, g_mid))

    done = jnp.concatenate([sum_d.value, sum_c.value, sum_b.value], axis=1)
    out_1 = Flow(completing(done, 4096))
    inputs_wide = inputs.astype(F32)
    g_add, g_gain_1 = rms_back(g_n1, inputs_wide, gain_1)
    g_hidden = g_mid + g_add
    top, rest = halves(g_hidden)
    grad_hidden = mm_nt(top, order) + mm_nt(rest, order)
    g_gains = jnp.dot(
        jnp.concatenate([g_gain_1, g_gain_2, jnp.zeros((6, width), F32)], axis=0),
        order.astype(F32).T, precision=HIGH,
    )
    g_skip = gate_sums[1].reshape(NH_SSM, HP).sum(axis=1)
    small = jnp.concatenate(
        [g_gains[:2].reshape(-1), g_taps[: KCONV + 1].reshape(-1), gate_sums[0], g_dt_bias, g_a_log, g_skip,
         jnp.zeros((LANES - 3 * NH_SSM,), F32)]
    )
    total = Flow(summing(small.reshape(-1, LANES)))
    grad_hidden = tick([sum_a1, sum_a2, out_1, total], grad_hidden)
    grad_hidden = tick([sum_a1, sum_a2, out_1, total], grad_hidden)
    flows = [sum_a2, total]
    while sum_a2.pending:
        grad_hidden = tick([f for f in (sum_a2, total) if f.pending], grad_hidden)
    out_2 = Flow(completing(jnp.concatenate([sum_a1.value, sum_a2.value], axis=1), 2176))
    while out_2.pending or total.pending:
        grad_hidden = tick([f for f in (out_2, total) if f.pending], grad_hidden)
    early, late = out_1.value, out_2.value
    small = total.value.reshape(-1)
    sizes = [width, width, KCONV * CONV, CONV, INNER, NH_SSM, NH_SSM, NH_SSM]
    starts = [sum(sizes[:k]) for k in range(len(sizes))]
    out_gain_1, out_gain_2, out_conv_w, out_conv_b, out_gain_s, out_dt_bias, out_a_log, out_skip = (
        small[at : at + size] for at, size in zip(starts, sizes)
    )
    return (
        out_hidden,
        grad_hidden,
        out_gain_1,
        late[:, :INNER],
        late[:, conv_at:dt_at],
        late[:, dt_at : dt_at + NH_SSM],
        out_conv_w.reshape(KCONV, CONV),
        out_conv_b,
        out_dt_bias,
        out_a_log,
        out_skip,
        out_gain_s,
        early[:, 3 * hidden : 3 * hidden + INNER].T,
        late[:, q_at:k_at],
        late[:, k_at:v_at],
        late[:, v_at:conv_at],
        early[:, 3 * hidden + INNER :].T,
        out_gain_2,
        early[:, hidden : 2 * hidden],
        early[:, 2 * hidden : 3 * hidden],
        early[:, :hidden].T,
    )


def solution(mesh):
    tokens = P(("rep", "fsdp", "seq"), None)
    wide, tall, same = P(("fsdp", "seq"), None), P(None, ("fsdp", "seq")), P()
    return jax.shard_map(
        body,
        mesh=mesh,
        in_specs=(
            tokens, same, wide, wide, wide, same, same, same, same, same, same, tall,
            wide, wide, wide, tall, same, wide, wide, tall, tokens,
        ),
        out_specs=(
            tokens, tokens, same, wide, wide, wide, same, same, same, same, same, same, tall,
            wide, wide, wide, tall, same, wide, wide, tall,
        ),
        check_vma=False,
    )
```

time: 1400 us -> 629 us (0.45)
  waiting for transfers between devices: 649 us -> 112 us
  matrix products: 307 us -> 103 us
  starting transfers between devices: 5.19 us -> 113 us
  blocking collectives: 95.5 us -> 2.18 us
  local copies, waits for them, and re-layouts: 198 us -> 111 us
  Pallas kernels: 0 us -> 71.3 us
    reduce_scatter x13 -> x0, waiting for transfers between devices: 555 us -> none  [the longest x1 88.4 us: body(): lax.psum_scatter(term_gate, ('fsdp', 'seq'), scatter_dimension=0, tiled=T...]
    dot_general x97 -> x37, matrix products: 296 us -> 103 us  [the longest x10 36.2 us: mm(): return jnp.dot(a, b, preferred_element_type=F32)]
    ppermute x0 -> x86, waiting for transfers between devices: none -> 112 us  [the longest x28 79.3 us: shifted(): lax.ppermute(value, axis, [(i, (i + by) % count) for i in range(count)])]
    ppermute x0 -> x86, starting transfers between devices: none -> 106 us  [the longest x58 54.3 us: trade(): return lax.ppermute(value, axis, [(i, i ^ bit) for i in range(count)])]
    dynamic_update_slice x8 -> x0, local copies, waits for them, and re-layouts: 83.1 us -> none  [ssd_local(): final_state, outputs = lax.scan(jax.checkpoint(ssd_block), initial, blocks)]
    psum x2 -> x0, waiting for transfers between devices: 75.1 us -> none  [the longest x1 75.1 us: body(): lax.psum(shard_z.astype(jnp.bfloat16), 'rep').astype(jnp.float32)]
    pallas_call x0 -> x6, Pallas kernels: none -> 71.3 us  [the longest x1 20.2 us: mixer_back(): pl.pallas_call(mixer_back_kernel, grid=(count,), in_specs=[back(INNER), b...]
    all_gather x7 -> x1, blocking collectives: 53.6 us -> 2.18 us  [body(): lax.all_gather(jnp.concatenate([k_low, proj[:, v_at:conv_at].astype(LOW)]...]
  transfers between devices with their start and end apart: 25 -> 90, of which waited for: 11 -> 22; matrix products, arithmetic and copies ran while one was open for 27% -> 34% of each run, Pallas kernels for 0% -> 10%
where the time goes in v1:
time: 629 us; the launch traced here: 617 us
  starting transfers between devices  113 us (18%)
  waiting for transfers between devices  112 us (18%)
  local copies, waits for them, and re-layouts  111 us (18%)
  matrix products  103 us (16%)
  other arithmetic  101 us (16%)
  Pallas kernels  71.3 us (11%)
    ppermute x28, waiting for transfers between devices, shifted(): lax.ppermute(value, axis, [(i, (i + by) % count) for i in range(count)])  79.3 us
    ppermute x58, starting transfers between devices, trade(): return lax.ppermute(value, axis, [(i, i ^ bit) for i in range(count)])  54.3 us
    ppermute x28, starting transfers between devices, shifted(): lax.ppermute(value, axis, [(i, (i + by) % count) for i in range(count)])  51.4 us
    unnamed x468, local copies, waits for them, and re-layouts  43.7 us
    dot_general x10, matrix products, mm(): return jnp.dot(a, b, preferred_element_type=F32)  36.2 us
    ppermute x58, waiting for transfers between devices, trade(): return lax.ppermute(value, axis, [(i, i ^ bit) for i in range(count)])  32.7 us
    dot_general x13, matrix products, mm_nt(): lax.dot_general(a, b, (((1,), (1,)), ((), ())), preferred_element_type=F32)  32 us
    dot_general x10, matrix products, mm_tn(): lax.dot_general(a, b, (((0,), (0,)), ((), ())), preferred_element_type=F32)  31.3 us
  transfers between devices with their start and end apart: 90, of which 22 were waited for; matrix products, arithmetic and copies ran while one was open for 34% of the time, Pallas kernels for 10%

profile of v1, /device:TPU:0, one launch (start us, length us, event | category | flops | bytes accessed | tf_op | source)
XLA Modules:
  0.0 617.4 jit_solution(8006536517480342343)
XLA Ops:
  55.1 6.3 %collective-permute-done.7 = bf16[32,2048]{0,1:T(8,128)(2,1)S(1)} collective-permute-done((bf16[32,2048]{0,1:T(8,128)(2,1)S(1)}, bf16[32,2048]{0,1:T(8,128)(2,1)S(1)}, u32[]{:S(2)}, u32[]{:S(2)}) %collective-permute-start.7) | collective-permute-done | bytes 131104 | tf_op jit(solution)/shard_map/ppermute | solution.py:556
  61.4 20.0 %collective-permute-done.8 = bf16[32,2048]{0,1:T(8,128)(2,1)S(1)} collective-permute-done((bf16[32,2048]{0,1:T(8,128)(2,1)S(1)}, bf16[32,2048]{0,1:T(8,128)(2,1)S(1)}, u32[]{:S(2)}, u32[]{:S(2)}) %collective-permute-start.8) | collective-permute-done | bytes 131104 | tf_op jit(solution)/shard_map/ppermute | solution.py:556
  88.8 11.0 %collective-permute-start.15 = (bf16[32,4096]{1,0:T(8,128)(2,1)}, bf16[32,4096]{1,0:T(8,128)(2,1)}, u32[]{:S(2)}, u32[]{:S(2)}) collective-permute-start(bf16[32,4096]{1,0:T(8,128)(2,1)} %constant_dynamic-slice_fusion.14), channel_id=1, source_target_pairs={{0,2},{2,4},{4,6},{6,0},{1,3},{3,5},{5,7},{7,1},{8,10},{10,12},{12... | collective-permute-start | bytes 786440 | tf_op jit(solution)/shard_map/ppermute | solution.py:556
  103.2 5.7 collective-permute-done.11
  111.7 4.9 fusion.106
  116.6 6.2 %fusion.212 = (bf16[512,4224]{1,0:T(8,128)(2,1)}, f32[512,4224]{1,0:T(8,128)S(1)}) fusion(f32[512,4224]{1,0:T(8,128)S(1)} %fusion.106, bf16[512,2048]{1,0:T(8,128)(2,1)} %copy-done.69, bf16[512,2176]{1,0:T(8,128)(2,1)S(1)} %copy-done.60, bf16[512,1024]{0,1:T(8,128)(2,1)S(1)} %copy-done.84), kind=kOutput, calls=%fused_computation.505 | convolution fusion | flops 2227568640 | bytes 26476544 | tf_op jit(solution)/shard_map/dot_general | solution.py:32
  138.0 5.3 mixer_states.1
  170.7 11.9 %attend.1 = (bf16[512,512]{1,0:T(8,128)(2,1)S(1)}, bf16[512,512]{1,0:T(8,128)(2,1)S(1)}, f32[4,8,512]{2,1,0:T(8,128)S(1)}) custom-call(s32[1]{0:T(128)} %bitcast.12.first_ref, f32[512,4224]{1,0:T(8,128)} %copy-done.37, f32[512,128]{1,0:T(8,128)S(1)} %get-tuple-element.212.cos_ref, f32[512,128]{1,0:T(8,128)S(1)} %get-tuple-element.213.sin_ref, ...), custom_call_target="tpu_custom_call" | custom-call | tf_op jit(solution)/shard_map/attend/pallas_call | solution.py:506
  191.8 8.5 %mixer_forward.1 = (bf16[512,1536]{1,0:T(8,128)(2,1)S(1)}, f32[512,1536]{1,0:T(8,128)S(1)}, bf16[4,128,1536]{2,1,0:T(8,128)(2,1)S(1)}, bf16[4,128,1536]{2,1,0:T(8,128)(2,1)S(1)}) custom-call(f32[512,1792]{1,0:T(8,128)S(1)} %copy-done.3, f32[512,128]{1,0:T(8,128)S(1)} %copy-done.18, f32[512,128]{1,0:T(8,128)S(1)} %bitcast.303, f32[512,128]{1,0:T(8,128)S(1)} %bitcast.306, ...), custom_call_target="tpu_custom_call" | custom-call | tf_op jit(solution)/shard_map/mixer_forward/pallas_call | solution.py:333
  203.1 6.6 %collective-permute-done.26 = bf16[32,2048]{0,1:T(8,128)(2,1)} collective-permute-done((bf16[32,2048]{0,1:T(8,128)(2,1)S(1)}, bf16[32,2048]{0,1:T(8,128)(2,1)}, u32[]{:S(2)}, u32[]{:S(2)}) %collective-permute-start.26) | collective-permute-done | bytes 131104 | tf_op jit(solution)/shard_map/ppermute | solution.py:556
  240.4 6.8 %collective-permute-done.32 = bf16[192,1024]{0,1:T(8,128)(2,1)S(1)} collective-permute-done((bf16[192,1024]{0,1:T(8,128)(2,1)S(1)}, bf16[192,1024]{0,1:T(8,128)(2,1)S(1)}, u32[]{:S(2)}, u32[]{:S(2)}) %collective-permute-start.32) | collective-permute-done | bytes 393248 | tf_op jit(solution)/shard_map/ppermute | solution.py:551
  272.8 5.6 multiply_convert_fusion.1
  308.4 5.2 convolution_add_fusion.3.g_ref
  314.4 6.7 %gate_back.1 = (bf16[512,1536]{1,0:T(8,128)(2,1)S(1)}, bf16[512,1536]{1,0:T(8,128)(2,1)S(1)}, f32[8,1536]{1,0:T(8,128)S(1)}, f32[128,1536]{1,0:T(8,128)S(1)}) custom-call(f32[512,2048]{1,0:T(8,128)} %convolution_add_fusion.3.g_ref, f32[512,1536]{1,0:T(8,128)S(1)} %get-tuple-element.265.y_ref, f32[512,1792]{1,0:T(8,128)S(1)} %copy-done.4, ...), custom_call_target="tpu_custom_call" | custom-call | tf_op jit(solution)/shard_map/gate_back/pallas_call | solution.py:358
  328.2 4.5 convert_add_fusion
  349.6 18.7 %attend_back.1 = (bf16[512,512]{1,0:T(8,128)(2,1)S(1)}, f32[1024,256]{1,0:T(8,128)S(1)}) custom-call(s32[1]{0:T(128)} %bitcast.12.first_ref, f32[512,2048]{1,0:T(8,128)} %convolution_add_fusion.3.g_ref, bf16[512,512]{1,0:T(8,128)(2,1)S(1)} %copy-done.30, f32[512,128]{1,0:T(8,128)S(1)} %copy-done.14, f32[512,128]{1,0:T(8,128)S(1)} %copy-done.12, ...), custom_call_target="tpu_custom_call" | custom-call | tf_op jit(solution)/shard_map/attend_back/pallas_call | solution.py:527
  382.3 13.0 %collective-permute-start.44 = (bf16[32,2048]{1,0:T(8,128)(2,1)S(1)}, bf16[32,2048]{1,0:T(8,128)(2,1)S(1)}, u32[]{:S(2)}, u32[]{:S(2)}) collective-permute-start(bf16[32,2048]{1,0:T(8,128)(2,1)S(1)} %get-tuple-element.506), channel_id=1, source_target_pairs={{0,6},{2,0},{4,2},{6,4},{1,7},{3,1},{5,3},{7,5},{8,14},{10,8},{12,... | collective-permute-start | bytes 393224 | tf_op jit(solution)/shard_map/ppermute | solution.py:556
  399.7 6.8 %collective-permute-done.45 = bf16[32,2048]{1,0:T(8,128)(2,1)S(1)} collective-permute-done((bf16[32,2048]{1,0:T(8,128)(2,1)S(1)}, bf16[32,2048]{1,0:T(8,128)(2,1)S(1)}, u32[]{:S(2)}, u32[]{:S(2)}) %collective-permute-start.45) | collective-permute-done | bytes 131104 | tf_op jit(solution)/shard_map/ppermute | solution.py:556
  407.4 6.6 %collective-permute-done.46 = bf16[32,2048]{1,0:T(8,128)(2,1)S(1)} collective-permute-done((bf16[32,2048]{1,0:T(8,128)(2,1)S(1)}, bf16[32,2048]{1,0:T(8,128)(2,1)S(1)}, u32[]{:S(2)}, u32[]{:S(2)}) %collective-permute-start.46) | collective-permute-done | bytes 131104 | tf_op jit(solution)/shard_map/ppermute | solution.py:556
  424.5 20.2 %mixer_back.1 = (bf16[512,1792]{1,0:T(8,128)(2,1)}, f32[8,1792]{1,0:T(8,128)S(1)}, f32[8,1792]{1,0:T(8,128)S(1)}, f32[512,128]{1,0:T(8,128)S(1)}, f32[512,128]{1...) custom-call(bf16[512,1536]{1,0:T(8,128)(2,1)S(1)} %copy-done.26, f32[512,1536]{1,0:T(8,128)} %copy-done.6, ...), custom_call_target="tpu_custom_call" | custom-call | tf_op jit(solution)/shard_map/mixer_back/pallas_call | solution.py:384
  445.2 9.4 %collective-permute-done.54 = bf16[32,4096]{1,0:T(8,128)(2,1)S(1)} collective-permute-done((bf16[32,4096]{1,0:T(8,128)(2,1)S(1)}, bf16[32,4096]{1,0:T(8,128)(2,1)S(1)}, u32[]{:S(2)}, u32[]{:S(2)}) %collective-permute-start.54) | collective-permute-done | bytes 262176 | tf_op jit(solution)/shard_map/ppermute | solution.py:556
  484.2 6.1 collective-permute-done.60
  517.9 10.6 %collective-permute-done.65 = bf16[128,1152]{1,0:T(8,128)(2,1)S(1)} collective-permute-done((bf16[128,1152]{1,0:T(8,128)(2,1)S(1)}, bf16[128,1152]{1,0:T(8,128)(2,1)S(1)}, u32[]{:S(2)}, u32[]{:S(2)}) %collective-permute-start.65) | collective-permute-done | bytes 294944 | tf_op jit(solution)/shard_map/ppermute | solution.py:551
  548.6 6.7 %collective-permute-done.74 = bf16[32,2304]{1,0:T(8,128)(2,1)S(1)} collective-permute-done((bf16[32,2304]{1,0:T(8,128)(2,1)}, bf16[32,2304]{1,0:T(8,128)(2,1)S(1)}, u32[]{:S(2)}, u32[]{:S(2)}) %collective-permute-start.74) | collective-permute-done | bytes 147488 | tf_op jit(solution)/shard_map/ppermute | solution.py:556
  (881 shorter events, 400.1 us)
Async XLA Ops:
  7.0 31.1 %collective-permute-start = (bf16[32,4224]{1,0:T(8,128)(2,1)}, bf16[32,4224]{1,0:T(8,128)(2,1)}, u32[]{:S(2)}, u32[]{:S(2)}) collective-permute-start(bf16[32,4224]{1,0:T(8,128)(2,1)} %constant_dynamic-slice_fusion.19), channel_id=1, source_target_pairs={{0,2},{2,4},{4,6},{6,0},{1,3},{3,5},{5,7},{7,1},{8,10},{10,12},{12... | collective-permute-start | bytes 811016 | tf_op jit(solution)/shard_map/ppermute | solution.py:556
  10.0 28.1 %collective-permute-start.1 = (bf16[32,4224]{1,0:T(8,128)(2,1)}, bf16[32,4224]{1,0:T(8,128)(2,1)}, u32[]{:S(2)}, u32[]{:S(2)}) collective-permute-start(bf16[32,4224]{1,0:T(8,128)(2,1)} %constant_dynamic-slice_fusion.19), channel_id=1, source_target_pairs={{0,4},{2,6},{4,0},{6,2},{1,5},{3,7},{5,1},{7,3},{8,12},{10,14},{12... | collective-permute-start | bytes 811016 | tf_op jit(solution)/shard_map/ppermute | solution.py:556
  45.3 36.1 %collective-permute-start.8 = (bf16[32,2048]{0,1:T(8,128)(2,1)S(1)}, bf16[32,2048]{0,1:T(8,128)(2,1)S(1)}, u32[]{:S(2)}, u32[]{:S(2)}) collective-permute-start(bf16[32,2048]{0,1:T(8,128)(2,1)S(1)} %constant_dynamic-slice_fusion.17), channel_id=1, source_target_pairs={{0,4},{2,6},{4,0},{6,2},{1,5},{3,7},{5,1},{7,3},{8,12},{10,14},{12... | collective-permute-start | bytes 393224 | tf_op jit(solution)/shard_map/ppermute | solution.py:556
  45.7 35.7 %collective-permute-start.9 = (bf16[32,2048]{0,1:T(8,128)(2,1)S(1)}, bf16[32,2048]{0,1:T(8,128)(2,1)S(1)}, u32[]{:S(2)}, u32[]{:S(2)}) collective-permute-start(bf16[32,2048]{0,1:T(8,128)(2,1)S(1)} %constant_dynamic-slice_fusion.17), channel_id=1, source_target_pairs={{0,6},{2,0},{4,2},{6,4},{1,7},{3,1},{5,3},{7,5},{8,14},{10,8},{12,... | collective-permute-start | bytes 393224 | tf_op jit(solution)/shard_map/ppermute | solution.py:556
  52.7 28.7 %collective-permute-start.6 = (bf16[192,2048]{1,0:T(8,128)(2,1)S(1)}, bf16[192,2048]{1,0:T(8,128)(2,1)S(1)}, u32[]{:S(2)}, u32[]{:S(2)}) collective-permute-start(bf16[192,2048]{1,0:T(8,128)(2,1)S(1)} %pad_maximum_fusion.20), channel_id=1, source_target_pairs={{0,8},{8,0},{16,24},{24,16},{1,9},{9,1},{17,25},{25,17},{2,10},{10... | collective-permute-start | bytes 2359304 | tf_op jit(solution)/shard_map/ppermute | solution.py:551
  53.5 27.9 %collective-permute-start.5 = (bf16[192,2176]{1,0:T(8,128)(2,1)S(1)}, bf16[192,2176]{1,0:T(8,128)(2,1)S(1)}, u32[]{:S(2)}, u32[]{:S(2)}) collective-permute-start(bf16[192,2176]{1,0:T(8,128)(2,1)S(1)} %pad_maximum_fusion.19), channel_id=1, source_target_pairs={{0,16},{8,24},{16,0},{24,8},{1,17},{9,25},{17,1},{25,9},{2,18},{10... | collective-permute-start | bytes 2506760 | tf_op jit(solution)/shard_map/ppermute | solution.py:551
  88.8 56.2 %collective-permute-start.15 = (bf16[32,4096]{1,0:T(8,128)(2,1)}, bf16[32,4096]{1,0:T(8,128)(2,1)}, u32[]{:S(2)}, u32[]{:S(2)}) collective-permute-start(bf16[32,4096]{1,0:T(8,128)(2,1)} %constant_dynamic-slice_fusion.14), channel_id=1, source_target_pairs={{0,2},{2,4},{4,6},{6,0},{1,3},{3,5},{5,7},{7,1},{8,10},{10,12},{12... | collective-permute-start | bytes 786440 | tf_op jit(solution)/shard_map/ppermute | solution.py:556
  99.8 45.3 %collective-permute-start.16 = (bf16[32,4096]{1,0:T(8,128)(2,1)}, bf16[32,4096]{1,0:T(8,128)(2,1)}, u32[]{:S(2)}, u32[]{:S(2)}) collective-permute-start(bf16[32,4096]{1,0:T(8,128)(2,1)} %constant_dynamic-slice_fusion.14), channel_id=1, source_target_pairs={{0,4},{2,6},{4,0},{6,2},{1,5},{3,7},{5,1},{7,3},{8,12},{10,14},{12... | collective-permute-start | bytes 786440 | tf_op jit(solution)/shard_map/ppermute | solution.py:556
  108.9 36.2 %collective-permute-start.17 = (bf16[32,4096]{1,0:T(8,128)(2,1)}, bf16[32,4096]{1,0:T(8,128)(2,1)}, u32[]{:S(2)}, u32[]{:S(2)}) collective-permute-start(bf16[32,4096]{1,0:T(8,128)(2,1)} %constant_dynamic-slice_fusion.14), channel_id=1, source_target_pairs={{0,6},{2,0},{4,2},{6,4},{1,7},{3,1},{5,3},{7,5},{8,14},{10,8},{12,... | collective-permute-start | bytes 786440 | tf_op jit(solution)/shard_map/ppermute | solution.py:556
  145.9 36.8 %collective-permute-start.22 = (bf16[128,1536]{1,0:T(8,128)(2,1)}, bf16[128,1536]{1,0:T(8,128)(2,1)}, u32[]{:S(2)}, u32[]{:S(2)}) collective-permute-start(bf16[128,1536]{1,0:T(8,128)(2,1)} %add_convert_fusion.1), channel_id=1, source_target_pairs={{0,1},{2,3},{4,5},{6,7},{8,9},{10,11},{12,13},{14,15},{16,17},{18,... | collective-permute-start | bytes 1179656 | tf_op jit(solution)/shard_map/ppermute | solution.py:562
  170.6 32.5 %collective-permute-start.25 = (bf16[32,2048]{0,1:T(8,128)(2,1)S(1)}, bf16[32,2048]{0,1:T(8,128)(2,1)}, u32[]{:S(2)}, u32[]{:S(2)}) collective-permute-start(bf16[32,2048]{0,1:T(8,128)(2,1)S(1)} %constant_dynamic-slice_fusion.15), channel_id=1, source_target_pairs={{0,2},{2,4},{4,6},{6,0},{1,3},{3,5},{5,7},{7,1},{8,10},{10,12},{12... | collective-permute-start | bytes 393224 | tf_op jit(solution)/shard_map/ppermute | solution.py:556
  182.7 27.0 %collective-permute-start.26 = (bf16[32,2048]{0,1:T(8,128)(2,1)S(1)}, bf16[32,2048]{0,1:T(8,128)(2,1)}, u32[]{:S(2)}, u32[]{:S(2)}) collective-permute-start(bf16[32,2048]{0,1:T(8,128)(2,1)S(1)} %constant_dynamic-slice_fusion.15), channel_id=1, source_target_pairs={{0,4},{2,6},{4,0},{6,2},{1,5},{3,7},{5,1},{7,3},{8,12},{10,14},{12... | collective-permute-start | bytes 393224 | tf_op jit(solution)/shard_map/ppermute | solution.py:556
  285.0 28.6 %collective-permute-start.37 = (bf16[512,4096]{1,0:T(8,128)(2,1)}, bf16[512,4096]{1,0:T(8,128)(2,1)}, u32[]{:S(2)}, u32[]{:S(2)}) collective-permute-start(bf16[512,4096]{1,0:T(8,128)(2,1)} %convolution_convert_fusion), channel_id=1, source_target_pairs={{0,1},{1,0},{2,3},{3,2},{4,5},{5,4},{6,7},{7,6},{8,9},{9,8},{10,11... | collective-permute-start | bytes 12582920 | tf_op jit(solution)/shard_map/ppermute | solution.py:551
  326.2 44.5 %collective-permute-start.42 = (bf16[512,2048]{1,0:T(8,128)(2,1)}, bf16[512,2048]{1,0:T(8,128)(2,1)}, u32[]{:S(2)}, u32[]{:S(2)}) collective-permute-start(bf16[512,2048]{1,0:T(8,128)(2,1)} %convolution_convert_fusion.3), channel_id=1, source_target_pairs={{0,1},{1,0},{2,3},{3,2},{4,5},{5,4},{6,7},{7,6},{8,9},{9,8},{10,11... | collective-permute-start | bytes 6291464 | tf_op jit(solution)/shard_map/ppermute | solution.py:551
  337.3 33.4 %collective-permute-start.41 = (bf16[256,2048]{1,0:T(8,128)(2,1)}, bf16[256,2048]{1,0:T(8,128)(2,1)}, u32[]{:S(2)}, u32[]{:S(2)}) collective-permute-start(bf16[256,2048]{1,0:T(8,128)(2,1)} %pad_maximum_fusion.16), channel_id=1, source_target_pairs={{0,16},{8,24},{16,0},{24,8},{1,17},{9,25},{17,1},{25,9},{2,18},{10... | collective-permute-start | bytes 3145736 | tf_op jit(solution)/shard_map/ppermute | solution.py:551
  339.9 30.7 %collective-permute-start.40 = (bf16[256,2048]{1,0:T(8,128)(2,1)}, bf16[256,2048]{1,0:T(8,128)(2,1)}, u32[]{:S(2)}, u32[]{:S(2)}) collective-permute-start(bf16[256,2048]{1,0:T(8,128)(2,1)} %pad_maximum_fusion.15), channel_id=1, source_target_pairs={{0,8},{8,0},{16,24},{24,16},{1,9},{9,1},{17,25},{25,17},{2,10},{10... | collective-permute-start | bytes 3145736 | tf_op jit(solution)/shard_map/ppermute | solution.py:551
  343.8 26.9 %collective-permute-start.39 = (bf16[128,1024]{1,0:T(8,128)(2,1)}, bf16[128,1024]{1,0:T(8,128)(2,1)}, u32[]{:S(2)}, u32[]{:S(2)}) collective-permute-start(bf16[128,1024]{1,0:T(8,128)(2,1)} %get-tuple-element.439), channel_id=1, source_target_pairs={{0,8},{8,0},{16,24},{24,16},{1,9},{9,1},{17,25},{25,17},{2,10},{10... | collective-permute-start | bytes 786440 | tf_op jit(solution)/shard_map/ppermute | solution.py:551
  374.4 39.5 %collective-permute-start.50 = (bf16[256,1024]{1,0:T(8,128)(2,1)S(1)}, bf16[256,1024]{1,0:T(8,128)(2,1)S(1)}, u32[]{:S(2)}, u32[]{:S(2)}) collective-permute-start(bf16[256,1024]{1,0:T(8,128)(2,1)S(1)} %pad_maximum_fusion.41), channel_id=1, source_target_pairs={{0,16},{8,24},{16,0},{24,8},{1,17},{9,25},{17,1},{25,9},{2,18},{10... | collective-permute-start | bytes 1572872 | tf_op jit(solution)/shard_map/ppermute | solution.py:551
  375.1 38.9 %collective-permute-start.49 = (bf16[256,1024]{1,0:T(8,128)(2,1)S(1)}, bf16[256,1024]{1,0:T(8,128)(2,1)S(1)}, u32[]{:S(2)}, u32[]{:S(2)}) collective-permute-start(bf16[256,1024]{1,0:T(8,128)(2,1)S(1)} %pad_maximum_fusion.40), channel_id=1, source_target_pairs={{0,8},{8,0},{16,24},{24,16},{1,9},{9,1},{17,25},{25,17},{2,10},{10... | collective-permute-start | bytes 1572872 | tf_op jit(solution)/shard_map/ppermute | solution.py:551
  379.1 34.8 %collective-permute-start.47 = (bf16[128,2048]{1,0:T(8,128)(2,1)S(1)}, bf16[128,2048]{1,0:T(8,128)(2,1)S(1)}, u32[]{:S(2)}, u32[]{:S(2)}) collective-permute-start(bf16[128,2048]{1,0:T(8,128)(2,1)S(1)} %get-tuple-element.424), channel_id=1, source_target_pairs={{0,16},{8,24},{16,0},{24,8},{1,17},{9,25},{17,1},{25,9},{2,18},{10... | collective-permute-start | bytes 1572872 | tf_op jit(solution)/shard_map/ppermute | solution.py:551
  379.7 34.3 %collective-permute-start.48 = (bf16[128,2048]{1,0:T(8,128)(2,1)S(1)}, bf16[128,2048]{1,0:T(8,128)(2,1)S(1)}, u32[]{:S(2)}, u32[]{:S(2)}) collective-permute-start(bf16[128,2048]{1,0:T(8,128)(2,1)S(1)} %get-tuple-element.423), channel_id=1, source_target_pairs={{0,8},{8,0},{16,24},{24,16},{1,9},{9,1},{17,25},{25,17},{2,10},{10... | collective-permute-start | bytes 1572872 | tf_op jit(solution)/shard_map/ppermute | solution.py:551
  416.7 37.9 %collective-permute-start.57 = (bf16[512,2304]{1,0:T(8,128)(2,1)}, bf16[512,2304]{1,0:T(8,128)(2,1)}, u32[]{:S(2)}, u32[]{:S(2)}) collective-permute-start(bf16[512,2304]{1,0:T(8,128)(2,1)} %convolution_convert_fusion.1), channel_id=1, source_target_pairs={{0,1},{1,0},{2,3},{3,2},{4,5},{5,4},{6,7},{7,6},{8,9},{9,8},{10,11... | collective-permute-start | bytes 7077896 | tf_op jit(solution)/shard_map/ppermute | solution.py:551
  417.7 27.0 %collective-permute-start.55 = (bf16[128,1024]{1,0:T(8,128)(2,1)}, bf16[128,1024]{1,0:T(8,128)(2,1)S(1)}, u32[]{:S(2)}, u32[]{:S(2)}) collective-permute-start(bf16[128,1024]{1,0:T(8,128)(2,1)} %get-tuple-element.432), channel_id=1, source_target_pairs={{0,16},{8,24},{16,0},{24,8},{1,17},{9,25},{17,1},{25,9},{2,18},{10... | collective-permute-start | bytes 786440 | tf_op jit(solution)/shard_map/ppermute | solution.py:551
  462.4 27.9 %collective-permute-start.62 = (bf16[256,1152]{1,0:T(8,128)(2,1)}, bf16[256,1152]{1,0:T(8,128)(2,1)}, u32[]{:S(2)}, u32[]{:S(2)}) collective-permute-start(bf16[256,1152]{1,0:T(8,128)(2,1)} %pad_maximum_fusion.24), channel_id=1, source_target_pairs={{0,16},{8,24},{16,0},{24,8},{1,17},{9,25},{17,1},{25,9},{2,18},{10... | collective-permute-start | bytes 1769480 | tf_op jit(solution)/shard_map/ppermute | solution.py:551
  (280 other events, 3101.7 us)
